TPU v7x, 32 devices: a whole 2x2x4 slice. The times are simulated.
32 devices in a mesh: groups: 2 (over y), gz: 4 (over z), gy: 2 (over x), gx: 2 (over core).
Axes of the slice: x: 2, y: 2, z: 4, core: 2. Of those that a mesh axis runs over, the one named last changes fastest.
Arguments:
- populations: float32 [19, 32, 32, 512], P(None, ('groups', 'gx'), 'gy', 'gz'), parts along dimension 1, as said below
- displacement: float32 [3, 164352], P(None, ('groups', 'gz', 'gy', 'gx')), parts along dimension 1, may hold values from -0.18 to 0.18
- stiffness: float32 [256], P(('groups', 'gz', 'gy', 'gx')), parts along dimension 0, may hold values from 0.5 to 8
- base_node: int32 [3, 164352], P(None, ('groups', 'gz', 'gy', 'gx')), parts along dimension 1, may hold values from 1 to 124, as said below
- offset: float32 [3, 164352], P(None, ('groups', 'gz', 'gy', 'gx')), parts along dimension 1, may hold values from 0 to 1
- destination: int32 [164352, 1], P(('groups', 'gz', 'gy', 'gx')), parts along dimension 0, may hold values from 0 to 7; in each aligned block of 5136 rows (0 to 5135, 5136 to 10271, ...) at most 1284 rows name the same one
Outputs:
- new_populations: float32 [19, 32, 32, 512], P(None, ('groups', 'gx'), 'gy', 'gz'), parts along dimension 1
- marker_velocity: float32 [3, 164352], P(None, ('groups', 'gz', 'gy', 'gx')), parts along dimension 1
There are 2 independent parts, one for each index of `groups`. A program takes and returns all parts, laid end to end along the dimension named above; each array names one. Nothing has to cross between parts.
Inputs may be any that keep to these rules, and one draw needn't show every extreme that they name: `base_node`: row 0 lies in 1 .. 4, row 1 in 1 .. 12, row 2 in 1 .. 124, so that every kernel node lies in the destination brick. The rows of one device name each destination at most 1284 times; in every draw some device names some destination exactly 1284 times. `populations`: every population lies between one half and one and a half times its lattice weight.
All inputs are finite; a program needn't handle non-finite values.
Results may differ from a plain program's by a relative error of at most 0.0003.
Values sent between devices are 32-bit elements; how exact they have to be, the bound alone decides.
A program may use at most 64 MiB of HBM per device.

v0:
```python
import math

import jax
import jax.numpy as jnp
import numpy as np
from jax import lax
from jax.sharding import PartitionSpec as P

LATTICE = np.array(
    [
        [0, 0, 0],
        [1, 0, 0],
        [-1, 0, 0],
        [0, 1, 0],
        [0, -1, 0],
        [0, 0, 1],
        [0, 0, -1],
        [1, 1, 0],
        [-1, -1, 0],
        [1, -1, 0],
        [-1, 1, 0],
        [1, 0, 1],
        [-1, 0, -1],
        [1, 0, -1],
        [-1, 0, 1],
        [0, 1, 1],
        [0, -1, -1],
        [0, 1, -1],
        [0, -1, 1],
    ]
)
WEIGHTS = [1.0 / 3.0] + [1.0 / 18.0] * 6 + [1.0 / 36.0] * 12
RELAXATION = 0.8
VELOCITY_UNIT = 0.01


def padded_2(shard, sides, width):
    for axis, dim in sides:
        size, length = (lax.axis_size(axis), shard.shape[dim])
        up = [(i, (i + 1) % size) for i in range(size)]
        down = [(j, i) for i, j in up]
        last = lax.slice_in_dim(shard, length - width, length, axis=dim)
        initial = lax.slice_in_dim(shard, 0, width, axis=dim)
        before = lax.ppermute(last, axis, up)
        after = lax.ppermute(initial, axis, down)
        shard = jnp.concatenate([before, shard, after], axis=dim)
    return shard


def kernel(distance):
    return jnp.where(jnp.abs(distance) < 2.0, 0.25 * (1.0 + jnp.cos(0.5 * math.pi * distance)), 0.0)


def marker_forces(displacement, stiffness):
    grouped = displacement.reshape(3, stiffness.shape[0], -1)
    centred = grouped - jnp.mean(grouped, axis=2, keepdims=True)
    return (stiffness[None, :, None] * centred).reshape(3, -1)


def momentum_sum(populations, dimension):
    total = jnp.zeros_like(populations[0])
    for index in range(19):
        step_sign = int(LATTICE[index][dimension])
        if step_sign != 0:
            total = total + step_sign * populations[index]
    return total


def collide(populations, force_field):
    density = jnp.sum(populations, axis=0)
    velocity = [
        (momentum_sum(populations, dimension) + 0.5 * force_field[dimension]) / density
        for dimension in range(3)
    ]
    speed_squared = (
        velocity[0] * velocity[0] + velocity[1] * velocity[1] + velocity[2] * velocity[2]
    )
    factor = 1.0 - 0.5 / RELAXATION
    result = []
    for index in range(19):
        lattice_row = [int(value) for value in LATTICE[index]]
        along = jnp.zeros_like(density)
        for dimension in range(3):
            if lattice_row[dimension] != 0:
                along = along + lattice_row[dimension] * velocity[dimension]
        equilibrium = (
            WEIGHTS[index]
            * density
            * (1.0 + 3.0 * along + 4.5 * along * along - 1.5 * speed_squared)
        )
        source = jnp.zeros_like(density)
        for dimension in range(3):
            source = (
                source
                + (
                    3.0 * (lattice_row[dimension] - velocity[dimension])
                    + 9.0 * along * lattice_row[dimension]
                )
                * force_field[dimension]
            )
        result.append(
            populations[index]
            - (populations[index] - equilibrium) / RELAXATION
            + factor * WEIGHTS[index] * source
        )
    return jnp.stack(result)


def fluid_velocity(populations):
    density = jnp.sum(populations, axis=0)
    return jnp.stack([momentum_sum(populations, dimension) / density for dimension in range(3)])


def axis_weights(length, coordinate):
    node_grid = jnp.arange(length, dtype=jnp.int32).astype(jnp.float32)[:, None]
    return kernel(node_grid - coordinate[None, :])


def moving_rows(dimension):
    return [index for index in range(19) if int(LATTICE[index][dimension]) != 0]


def shift_along(field, padded, moving, dimension, length):
    pieces = [field[index] for index in range(19)]
    for slot_pos, index in enumerate(moving):
        first_cell = 1 - int(LATTICE[index][dimension])
        pieces[index] = lax.slice_in_dim(
            padded[slot_pos], first_cell, first_cell + length, axis=dimension
        )
    return jnp.stack(pieces)


def shards(populations, displacement, stiffness, base_node, offset, destination):
    size_x, size_y, size_z = (populations.shape[1], populations.shape[2], populations.shape[3])
    peer_count = lax.axis_size(("gz", "gy"))
    markers = displacement.shape[1]
    capacity = max(2, (2 * markers + peer_count - 1) // peer_count)
    forces = marker_forces(displacement, stiffness)
    position = base_node.astype(jnp.float32) + offset
    target = destination[:, 0]
    onehot = (target[:, None] == jnp.arange(peer_count, dtype=jnp.int32)[None, :]).astype(jnp.int32)
    rank_in_peer = jnp.sum(jnp.cumsum(onehot, axis=0) * onehot, axis=1) - 1
    slot_index = target * capacity + rank_in_peer
    payload = jnp.concatenate([forces, position], axis=0)
    outgoing = jnp.zeros((6, peer_count * capacity), jnp.float32).at[:, slot_index].set(payload)
    arrived = lax.all_to_all(outgoing, ("gz", "gy"), split_axis=1, concat_axis=1, tiled=True)
    slot_total = arrived.shape[1]
    weight_x = axis_weights(size_x, arrived[3])
    weight_y = axis_weights(size_y, arrived[4])
    weight_z = axis_weights(size_z, arrived[5])
    carried = arrived[0:3]

    def spread_plane(plane_weight):
        blended = (
            carried[:, None, :] * plane_weight[None, None, :] * weight_y[None, :, :]
        ).reshape(3 * size_y, slot_total)
        return lax.dot_general(
            blended,
            weight_z,
            (((1,), (1,)), ((), ())),
            precision=lax.Precision.HIGHEST,
            preferred_element_type=jnp.float32,
        )

    planes = lax.map(spread_plane, weight_x)
    force_field = jnp.transpose(planes.reshape(size_x, 3, size_y, size_z), (1, 0, 2, 3))
    post = collide(populations, force_field)
    moving = moving_rows(0)
    padded = padded_2(jnp.stack([post[index] for index in moving]), (("gx", 1),), 1)
    post = shift_along(post, padded, moving, 0, size_x)
    moving = moving_rows(1)
    padded = padded_2(jnp.stack([post[index] for index in moving]), (("gy", 2),), 1)
    post = shift_along(post, padded, moving, 1, size_y)
    moving = moving_rows(2)
    padded = padded_2(jnp.stack([post[index] for index in moving]), (("gz", 3),), 1)
    new_populations = shift_along(post, padded, moving, 2, size_z)
    velocity_planes = jnp.transpose(fluid_velocity(new_populations), (1, 0, 2, 3)).reshape(
        size_x, 3 * size_y, size_z
    )

    def sample_plane(total, inputs):
        plane, plane_weight = inputs
        partial_value = jnp.dot(
            plane, weight_z, precision=lax.Precision.HIGHEST, preferred_element_type=jnp.float32
        )
        across = jnp.sum(
            partial_value.reshape(3, size_y, slot_total) * weight_y[None, :, :], axis=1
        )
        return (total + across * plane_weight[None, :], None)

    sampled, unused = lax.scan(
        sample_plane, jnp.zeros((3, slot_total), jnp.float32), (velocity_planes, weight_x)
    )
    sampled = sampled / VELOCITY_UNIT
    returned = lax.all_to_all(sampled, ("gz", "gy"), split_axis=1, concat_axis=1, tiled=True)
    marker_velocity = returned[:, slot_index]
    return (new_populations, marker_velocity)


def solution(mesh):
    return jax.shard_map(
        shards,
        mesh=mesh,
        in_specs=(
            P(None, ("groups", "gx"), "gy", "gz"),
            P(None, ("groups", "gz", "gy", "gx")),
            P(("groups", "gz", "gy", "gx")),
            P(None, ("groups", "gz", "gy", "gx")),
            P(None, ("groups", "gz", "gy", "gx")),
            P(("groups", "gz", "gy", "gx"), None),
        ),
        out_specs=(P(None, ("groups", "gx"), "gy", "gz"), P(None, ("groups", "gz", "gy", "gx"))),
        check_vma=False,
    )
```

profile of v0, /device:TPU:0, one launch (start us, length us, event | category | flops | bytes accessed | tf_op | source)
XLA Modules:
  0.0 562.4 jit_solution(16745241845906675436)
XLA Ops:
  7.9 23.0 %scatter_custom_fusion = f32[6,10272]{0,1:T(8,128)} fusion(s32[5136]{0:T(1024)S(1)} %fusion.293, f32[5136,6]{1,0:T(8,128)S(1)} %copy.75, f32[]{:T(128)} %constant.123.clone.1), kind=kCustom, calls=%fused_computation.70 | custom fusion | bytes 246532 | tf_op jit(solution)/shard_map/scatter | solution.py:145
  35.7 7.3 %all-to-all-start = ((f32[6,8,1284]{2,0,1:T(8,128)}), f32[6,8,1284]{2,0,1:T(8,128)S(1)}, u32[]{:S(2)}, u32[]{:S(2)}) async-start(f32[6,8,1284]{2,0,1:T(8,128)} %copy.77), calls=%async_computation | async-start | bytes 720896 | tf_op jit(solution)/shard_map/all_to_all | solution.py:146
  43.1 10.9 %all-to-all-done = f32[6,8,1284]{2,0,1:T(8,128)S(1)} async-done(((f32[6,8,1284]{2,0,1:T(8,128)}), f32[6,8,1284]{2,0,1:T(8,128)S(1)}, u32[]{:S(2)}, u32[]{:S(2)}) %all-to-all-start) | async-done | bytes 246560 | tf_op jit(solution)/shard_map/all_to_all | solution.py:146
  56.0 207.9 %while.22 = (s32[]{:T(128)}, f32[8,48,128]{2,1,0:T(8,128)S(1)}, f32[8,10272]{1,0:T(8,128)S(1)}, f32[3,10272]{1,0:T(4,128)S(1)}, f32[10272]{0:T(1024)S(1)}, /*ind...) while((s32[]{:T(128)}, f32[8,48,128]{2,1,0:T(8,128)S(1)}, ...), condition=%wide.region_7.8_spmd.clone, body=%wide.region_6.7_spmd.clone.sunk | while | flops 768212096 | bytes 5882157 | solution.py:165
  58.9 23.3 %fusion.314 = f32[8,48,128]{2,1,0:T(8,128)S(1)} fusion(f32[8,48,128]{2,1,0:T(8,128)S(1)} %get-tuple-element.323, s32[]{:T(128)S(6)} %copy.118, f32[48,10272]{1,0:T(8,128)S(1)} %bitcast.703, f32[10272]{0:T(1024)S(1)} %get-tuple-element.337, f32[128]{0:T(128)S(1)} %get-tuple-element.338), kind=kOutput, calls=%fused_computation.22.clone.1 | convolution fusion | flops 766537728 | bytes 2060804 | tf_op jit(solution)/shard_map/while/body/eval_jaxpr/dot_general | solution.py:157
  84.8 23.3 %fusion.314 = f32[8,48,128]{2,1,0:T(8,128)S(1)} fusion(f32[8,48,128]{2,1,0:T(8,128)S(1)} %get-tuple-element.323, s32[]{:T(128)S(6)} %copy.118, f32[48,10272]{1,0:T(8,128)S(1)} %bitcast.703, f32[10272]{0:T(1024)S(1)} %get-tuple-element.337, f32[128]{0:T(128)S(1)} %get-tuple-element.338), kind=kOutput, calls=%fused_computation.22.clone.1 | convolution fusion | flops 766537728 | bytes 2060804 | tf_op jit(solution)/shard_map/while/body/eval_jaxpr/dot_general | solution.py:157
  110.8 23.3 %fusion.314 = f32[8,48,128]{2,1,0:T(8,128)S(1)} fusion(f32[8,48,128]{2,1,0:T(8,128)S(1)} %get-tuple-element.323, s32[]{:T(128)S(6)} %copy.118, f32[48,10272]{1,0:T(8,128)S(1)} %bitcast.703, f32[10272]{0:T(1024)S(1)} %get-tuple-element.337, f32[128]{0:T(128)S(1)} %get-tuple-element.338), kind=kOutput, calls=%fused_computation.22.clone.1 | convolution fusion | flops 766537728 | bytes 2060804 | tf_op jit(solution)/shard_map/while/body/eval_jaxpr/dot_general | solution.py:157
  136.7 23.3 %fusion.314 = f32[8,48,128]{2,1,0:T(8,128)S(1)} fusion(f32[8,48,128]{2,1,0:T(8,128)S(1)} %get-tuple-element.323, s32[]{:T(128)S(6)} %copy.118, f32[48,10272]{1,0:T(8,128)S(1)} %bitcast.703, f32[10272]{0:T(1024)S(1)} %get-tuple-element.337, f32[128]{0:T(128)S(1)} %get-tuple-element.338), kind=kOutput, calls=%fused_computation.22.clone.1 | convolution fusion | flops 766537728 | bytes 2060804 | tf_op jit(solution)/shard_map/while/body/eval_jaxpr/dot_general | solution.py:157
  162.6 23.3 %fusion.314 = f32[8,48,128]{2,1,0:T(8,128)S(1)} fusion(f32[8,48,128]{2,1,0:T(8,128)S(1)} %get-tuple-element.323, s32[]{:T(128)S(6)} %copy.118, f32[48,10272]{1,0:T(8,128)S(1)} %bitcast.703, f32[10272]{0:T(1024)S(1)} %get-tuple-element.337, f32[128]{0:T(128)S(1)} %get-tuple-element.338), kind=kOutput, calls=%fused_computation.22.clone.1 | convolution fusion | flops 766537728 | bytes 2060804 | tf_op jit(solution)/shard_map/while/body/eval_jaxpr/dot_general | solution.py:157
  188.6 23.3 %fusion.314 = f32[8,48,128]{2,1,0:T(8,128)S(1)} fusion(f32[8,48,128]{2,1,0:T(8,128)S(1)} %get-tuple-element.323, s32[]{:T(128)S(6)} %copy.118, f32[48,10272]{1,0:T(8,128)S(1)} %bitcast.703, f32[10272]{0:T(1024)S(1)} %get-tuple-element.337, f32[128]{0:T(128)S(1)} %get-tuple-element.338), kind=kOutput, calls=%fused_computation.22.clone.1 | convolution fusion | flops 766537728 | bytes 2060804 | tf_op jit(solution)/shard_map/while/body/eval_jaxpr/dot_general | solution.py:157
  214.5 23.3 %fusion.314 = f32[8,48,128]{2,1,0:T(8,128)S(1)} fusion(f32[8,48,128]{2,1,0:T(8,128)S(1)} %get-tuple-element.323, s32[]{:T(128)S(6)} %copy.118, f32[48,10272]{1,0:T(8,128)S(1)} %bitcast.703, f32[10272]{0:T(1024)S(1)} %get-tuple-element.337, f32[128]{0:T(128)S(1)} %get-tuple-element.338), kind=kOutput, calls=%fused_computation.22.clone.1 | convolution fusion | flops 766537728 | bytes 2060804 | tf_op jit(solution)/shard_map/while/body/eval_jaxpr/dot_general | solution.py:157
  240.5 23.3 %fusion.314 = f32[8,48,128]{2,1,0:T(8,128)S(1)} fusion(f32[8,48,128]{2,1,0:T(8,128)S(1)} %get-tuple-element.323, s32[]{:T(128)S(6)} %copy.118, f32[48,10272]{1,0:T(8,128)S(1)} %bitcast.703, f32[10272]{0:T(1024)S(1)} %get-tuple-element.337, f32[128]{0:T(128)S(1)} %get-tuple-element.338), kind=kOutput, calls=%fused_computation.22.clone.1 | convolution fusion | flops 766537728 | bytes 2060804 | tf_op jit(solution)/shard_map/while/body/eval_jaxpr/dot_general | solution.py:157
  283.0 5.5 collective-permute-done.4
  298.3 236.0 %while.23 = (s32[]{:T(128)}, f32[3,10272]{1,0:T(4,128)S(1)}, f32[8,48,128]{2,1,0:T(8,128)S(1)}, f32[8,10272]{1,0:T(8,128)S(1)}, f32[10272]{0:T(1024)S(1)}, /*ind...) while((s32[]{:T(128)}, f32[3,10272]{1,0:T(4,128)S(1)}, ...), condition=%wide.region_10.11_spmd.clone, body=%wide.region_8.10_spmd.clone.sunk | while | flops 768735872 | bytes 2087743 | solution.py:191
  300.7 26.8 %fusion.318 = f32[3,10272]{1,0:T(4,128)S(1)} fusion(f32[3,16,128]{2,1,0:T(8,128)S(1)} %bitcast.706, f32[10272]{0:T(1024)S(1)} %get-tuple-element.364, f32[128]{0:T(128)S(1)} %get-tuple-element.365, f32[16,10272]{1,0:T(8,128)S(1)} %fusion.317), kind=kOutput, calls=%fused_computation.54.clone.1 | convolution fusion | flops 767492992 | bytes 846848 | tf_op jit(solution)/shard_map/while/body/eval_jaxpr/dot_general | solution.py:183
  330.2 26.8 %fusion.318 = f32[3,10272]{1,0:T(4,128)S(1)} fusion(f32[3,16,128]{2,1,0:T(8,128)S(1)} %bitcast.706, f32[10272]{0:T(1024)S(1)} %get-tuple-element.364, f32[128]{0:T(128)S(1)} %get-tuple-element.365, f32[16,10272]{1,0:T(8,128)S(1)} %fusion.317), kind=kOutput, calls=%fused_computation.54.clone.1 | convolution fusion | flops 767492992 | bytes 846848 | tf_op jit(solution)/shard_map/while/body/eval_jaxpr/dot_general | solution.py:183
  359.7 26.8 %fusion.318 = f32[3,10272]{1,0:T(4,128)S(1)} fusion(f32[3,16,128]{2,1,0:T(8,128)S(1)} %bitcast.706, f32[10272]{0:T(1024)S(1)} %get-tuple-element.364, f32[128]{0:T(128)S(1)} %get-tuple-element.365, f32[16,10272]{1,0:T(8,128)S(1)} %fusion.317), kind=kOutput, calls=%fused_computation.54.clone.1 | convolution fusion | flops 767492992 | bytes 846848 | tf_op jit(solution)/shard_map/while/body/eval_jaxpr/dot_general | solution.py:183
  389.2 26.8 %fusion.318 = f32[3,10272]{1,0:T(4,128)S(1)} fusion(f32[3,16,128]{2,1,0:T(8,128)S(1)} %bitcast.706, f32[10272]{0:T(1024)S(1)} %get-tuple-element.364, f32[128]{0:T(128)S(1)} %get-tuple-element.365, f32[16,10272]{1,0:T(8,128)S(1)} %fusion.317), kind=kOutput, calls=%fused_computation.54.clone.1 | convolution fusion | flops 767492992 | bytes 846848 | tf_op jit(solution)/shard_map/while/body/eval_jaxpr/dot_general | solution.py:183
  418.7 26.8 %fusion.318 = f32[3,10272]{1,0:T(4,128)S(1)} fusion(f32[3,16,128]{2,1,0:T(8,128)S(1)} %bitcast.706, f32[10272]{0:T(1024)S(1)} %get-tuple-element.364, f32[128]{0:T(128)S(1)} %get-tuple-element.365, f32[16,10272]{1,0:T(8,128)S(1)} %fusion.317), kind=kOutput, calls=%fused_computation.54.clone.1 | convolution fusion | flops 767492992 | bytes 846848 | tf_op jit(solution)/shard_map/while/body/eval_jaxpr/dot_general | solution.py:183
  448.2 26.8 %fusion.318 = f32[3,10272]{1,0:T(4,128)S(1)} fusion(f32[3,16,128]{2,1,0:T(8,128)S(1)} %bitcast.706, f32[10272]{0:T(1024)S(1)} %get-tuple-element.364, f32[128]{0:T(128)S(1)} %get-tuple-element.365, f32[16,10272]{1,0:T(8,128)S(1)} %fusion.317), kind=kOutput, calls=%fused_computation.54.clone.1 | convolution fusion | flops 767492992 | bytes 846848 | tf_op jit(solution)/shard_map/while/body/eval_jaxpr/dot_general | solution.py:183
  477.7 26.8 %fusion.318 = f32[3,10272]{1,0:T(4,128)S(1)} fusion(f32[3,16,128]{2,1,0:T(8,128)S(1)} %bitcast.706, f32[10272]{0:T(1024)S(1)} %get-tuple-element.364, f32[128]{0:T(128)S(1)} %get-tuple-element.365, f32[16,10272]{1,0:T(8,128)S(1)} %fusion.317), kind=kOutput, calls=%fused_computation.54.clone.1 | convolution fusion | flops 767492992 | bytes 846848 | tf_op jit(solution)/shard_map/while/body/eval_jaxpr/dot_general | solution.py:183
  507.3 26.8 %fusion.318 = f32[3,10272]{1,0:T(4,128)S(1)} fusion(f32[3,16,128]{2,1,0:T(8,128)S(1)} %bitcast.706, f32[10272]{0:T(1024)S(1)} %get-tuple-element.364, f32[128]{0:T(128)S(1)} %get-tuple-element.365, f32[16,10272]{1,0:T(8,128)S(1)} %fusion.317), kind=kOutput, calls=%fused_computation.54.clone.1 | convolution fusion | flops 767492992 | bytes 846848 | tf_op jit(solution)/shard_map/while/body/eval_jaxpr/dot_general | solution.py:183
  538.6 7.6 %all-to-all-done.1 = f32[3,8,1284]{2,0,1:T(4,128)S(1)} async-done(((f32[3,8,1284]{2,0,1:T(4,128)}), f32[3,8,1284]{2,0,1:T(4,128)S(1)}, u32[]{:S(2)}, u32[]{:S(2)}) %all-to-all-start.1) | async-done | bytes 123296 | tf_op jit(solution)/shard_map/all_to_all | solution.py:195
  549.8 11.1 %gather_fusion = f32[5136,3]{1,0:T(8,128)S(1)} fusion(f32[3,10272]{0,1:T(8,128)} %copy.108, s32[6144]{0:T(1024)S(1)} %pad_clamp_fusion), kind=kCustom, calls=%fused_computation | custom fusion | bytes 143808 | tf_op jit(solution)/shard_map/gather | solution.py:196
  (228 shorter events, 93.9 us)
Async XLA Ops:
  3.3 3.6 copy-start.13
  3.4 3.5 copy-start.7
  3.4 3.5 copy-start.14
  3.4 3.6 copy-start.15
  34.7 8.3 %copy-start = (f32[19,8,16,128]{3,2,1,0:T(8,128)S(1)}, f32[19,8,16,128]{3,2,1,0:T(8,128)}, u32[]{:S(2)}) copy-start(f32[19,8,16,128]{3,2,1,0:T(8,128)} %param.10) | copy-start | bytes 3735556
  35.7 18.3 %all-to-all-start = ((f32[6,8,1284]{2,0,1:T(8,128)}), f32[6,8,1284]{2,0,1:T(8,128)S(1)}, u32[]{:S(2)}, u32[]{:S(2)}) async-start(f32[6,8,1284]{2,0,1:T(8,128)} %copy.77), calls=%async_computation | async-start | bytes 720896 | tf_op jit(solution)/shard_map/all_to_all | solution.py:146
  264.0 1.0 copy-start.16
  264.0 1.0 copy-start.20
  266.0 1.3 collective-permute-start
  266.0 1.4 collective-permute-start.1
  268.6 4.1 collective-permute-start.2
  270.1 4.0 collective-permute-start.3
  276.5 6.5 %copy-start.12 = (s32[5136]{0:T(1024)S(1)}, s32[5136]{0:T(1024)}, u32[]{:S(2)}) copy-start(s32[5136]{0:T(1024)} %copy-done.11) | copy-start | bytes 61636
  281.0 9.7 %collective-permute-start.5 = (f32[10,8,16,1]{2,1,3,0:T(8,128)}, f32[10,8,16,1]{2,1,3,0:T(8,128)}, u32[]{:S(2)}, u32[]{:S(2)}) collective-permute-start(f32[10,8,16,1]{2,1,3,0:T(8,128)} %copy.102), channel_id=1, source_target_pairs={{4,0},{8,4},{12,8},{0,12},{5,1},{9,5},{13,9},{1,13},{6,2},{10,6},{... | collective-permute-start | bytes 15368 | tf_op jit(solution)/shard_map/ppermute | solution.py:45
  282.4 6.1 %collective-permute-start.4 = (f32[10,8,16,1]{2,1,3,0:T(8,128)}, f32[10,8,16,1]{2,1,3,0:T(8,128)}, u32[]{:S(2)}, u32[]{:S(2)}) collective-permute-start(f32[10,8,16,1]{2,1,3,0:T(8,128)} %copy.101), channel_id=1, source_target_pairs={{0,4},{4,8},{8,12},{12,0},{1,5},{5,9},{9,13},{13,1},{2,6},{6,10},{... | collective-permute-start | bytes 15368 | tf_op jit(solution)/shard_map/ppermute | solution.py:44
  294.8 1.0 copy-start.4
  294.8 1.1 copy-start.5
  294.8 1.1 copy-start.6
  294.8 1.1 copy-start.8
  294.8 1.1 copy-start.9
  294.8 1.1 copy-start.10
  296.1 1.3 copy-start.18
  535.2 11.0 %all-to-all-start.1 = ((f32[3,8,1284]{2,0,1:T(4,128)}), f32[3,8,1284]{2,0,1:T(4,128)S(1)}, u32[]{:S(2)}, u32[]{:S(2)}) async-start(f32[3,8,1284]{2,0,1:T(4,128)} %copy.106), calls=%async_computation.1 | async-start | bytes 360448 | tf_op jit(solution)/shard_map/all_to_all | solution.py:195
  538.6 7.8 %copy-start.19 = (f32[19,8,16,128]{3,2,1,0:T(8,128)}, f32[19,8,16,128]{3,2,1,0:T(8,128)S(1)}, u32[]{:S(2)}) copy-start(f32[19,8,16,128]{3,2,1,0:T(8,128)S(1)} %constant_dynamic-update-slice_fusion.30) | copy-start | bytes 3735556
  (6 other events, 5.3 us)
where the time goes:
time: 563 us; the launch traced here: 562 us
  matrix products  401 us (71%)
  local copies, waits for them, and re-layouts  64.7 us (11%)
  other arithmetic  51 us (9%)
  waiting for transfers between devices  28.3 us (5%)
  starting transfers between devices  15.3 us (3%)
    dot_general x8, matrix products, sample_plane(): jnp.dot(plane, weight_z, precision=lax.Precision.HIGHEST, preferred_eleme...  215 us
    dot_general x8, matrix products, spread_plane(): lax.dot_general(blended, weight_z, (((1,), (1,)), ((), ())), precision=la...  186 us
    select_n x17, other arithmetic, kernel(): jnp.where(jnp.abs(distance) < 2.0, 0.25 * (1.0 + jnp.cos(0.5 * math.pi *...  38.1 us
    scatter x2, local copies, waits for them, and re-layouts, shards(): jnp.zeros((6, peer_count * capacity), jnp.float32).at[:, slot_index]  26.8 us
  transfers between devices with their start and end apart: 8, of which 7 were waited for; matrix products, arithmetic and copies ran while one was open for 0% of the time, Pallas kernels for 0%

commit v1 on v0

--- a/solution.py
+++ b/solution.py
@@ -4,6 +4,8 @@
 import jax.numpy as jnp
 import numpy as np
 from jax import lax
+from jax.experimental import pallas as pl
+from jax.experimental.pallas import tpu as pltpu
 from jax.sharding import PartitionSpec as P
 
 LATTICE = np.array(
@@ -47,10 +49,6 @@
     return shard
 
 
-def kernel(distance):
-    return jnp.where(jnp.abs(distance) < 2.0, 0.25 * (1.0 + jnp.cos(0.5 * math.pi * distance)), 0.0)
-
-
 def marker_forces(displacement, stiffness):
     grouped = displacement.reshape(3, stiffness.shape[0], -1)
     centred = grouped - jnp.mean(grouped, axis=2, keepdims=True)
@@ -111,9 +109,271 @@
     return jnp.stack([momentum_sum(populations, dimension) / density for dimension in range(3)])
 
 
-def axis_weights(length, coordinate):
-    node_grid = jnp.arange(length, dtype=jnp.int32).astype(jnp.float32)[:, None]
-    return kernel(node_grid - coordinate[None, :])
+LANES = 128
+VMEM_LIMIT = 48 * 1024 * 1024
+NT = (((1,), (1,)), ((), ()))
+NN = (((1,), (0,)), ((), ()))
+
+
+def iota(shape, dimension):
+    return lax.broadcasted_iota(jnp.int32, shape, dimension)
+
+
+def split_two(value):
+    high = value.astype(jnp.bfloat16)
+    return high, (value - high.astype(jnp.float32)).astype(jnp.bfloat16)
+
+
+def route_kernel(peers, rows, target_ref, payload_ref, sent_ref, slot_ref, left_ref, right_ref):
+    chunks = target_ref.shape[0]
+    target = target_ref[...]
+    bf16 = jnp.bfloat16
+    upper = (iota((LANES, LANES), 0) < iota((LANES, LANES), 1)).astype(bf16)
+    lower = (iota((chunks, chunks), 1) < iota((chunks, chunks), 0)).astype(bf16)
+    ones = jnp.ones((LANES, LANES), bf16)
+
+    def ranked(peer, rank):
+        mask = target == peer
+        onehot = mask.astype(jnp.float32).astype(bf16)
+        within = lax.dot_general(onehot, upper, NN, preferred_element_type=jnp.float32)
+        ahead = lax.dot_general(lower, onehot, NN, preferred_element_type=jnp.float32)
+        before = lax.dot_general(ahead.astype(bf16), ones, NN, preferred_element_type=jnp.float32)
+        return jnp.where(mask, within + before, rank)
+
+    rank = lax.fori_loop(0, peers, ranked, jnp.zeros(target.shape, jnp.float32)).astype(jnp.int32)
+    slot_ref[0] = jnp.where(target < 0, -1, target * rows + lax.div(rank, LANES))
+    slot_ref[1] = lax.rem(rank, LANES)
+    height = left_ref.shape[0] // 15
+
+    def place(chunk, carry):
+        at = pl.ds(pl.multiple_of(chunk * LANES, LANES), LANES)
+        high_mask = iota((height, LANES), 0) == slot_ref[0, pl.ds(chunk, 1), :]
+        low_mask = iota((LANES, LANES), 0) == slot_ref[1, pl.ds(chunk, 1), :]
+        right_ref[:, at] = low_mask.astype(jnp.float32).astype(bf16)
+        values = payload_ref[:, at]
+        first = values.astype(bf16).astype(jnp.float32)
+        rest = values - first
+        second = rest.astype(bf16).astype(jnp.float32)
+        third = rest - second
+        piece = 0
+        for row in range(6):
+            for part in (first, second, third)[: 2 if row < 3 else 3]:
+                left_ref[piece * height : (piece + 1) * height, at] = jnp.where(
+                    high_mask, part[row : row + 1, :], 0.0
+                ).astype(bf16)
+                piece += 1
+        return carry
+
+    lax.fori_loop(0, chunks, place, 0)
+    placed = lax.dot_general(
+        left_ref[...], right_ref[...], NT, preferred_element_type=jnp.float32
+    )
+    piece = 0
+    for row in range(6):
+        count = 2 if row < 3 else 3
+        total = placed[piece * height : (piece + 1) * height]
+        for more in range(1, count):
+            total = total + placed[(piece + more) * height : (piece + more + 1) * height]
+        piece += count
+        for peer in range(peers):
+            sent_ref[peer, row * rows : (row + 1) * rows, :] = total[peer * rows : (peer + 1) * rows]
+
+
+def route(target, payload, peers, rows):
+    chunks = target.shape[0]
+    height = -(-peers * rows // 16) * 16
+    return pl.pallas_call(
+        lambda *refs: route_kernel(peers, rows, *refs),
+        out_shape=(
+            jax.ShapeDtypeStruct((peers, 6 * rows, LANES), jnp.float32),
+            jax.ShapeDtypeStruct((2, chunks, LANES), jnp.int32),
+        ),
+        scratch_shapes=[
+            pltpu.VMEM((15 * height, chunks * LANES), jnp.bfloat16),
+            pltpu.VMEM((LANES, chunks * LANES), jnp.bfloat16),
+        ],
+        compiler_params=pltpu.CompilerParams(vmem_limit_bytes=VMEM_LIMIT),
+        name="route",
+    )(target, payload)
+
+
+def stencil(position):
+    base = jnp.floor(position)
+    angle = (0.5 * math.pi) * (position - base)
+    sine, cosine = jnp.sin(angle), jnp.cos(angle)
+    weights = [0.25 - 0.25 * sine, 0.25 + 0.25 * cosine, 0.25 + 0.25 * sine, 0.25 - 0.25 * cosine]
+    return base.astype(jnp.int32), weights
+
+
+def node_weights(size, base, weights, row):
+    step = iota((size, LANES), 0) - base[row : row + 1, :]
+    result = jnp.zeros((size, LANES), jnp.float32)
+    for index in range(4):
+        result = jnp.where(step == index - 1, weights[index][row : row + 1, :], result)
+    return result
+
+
+def spread_kernel(sizes, rows, arrived_ref, field_ref, left_ref, right_ref, total_ref):
+    size_x, size_y, size_z = sizes
+    height = 3 * size_x * size_y
+    total_ref[...] = jnp.zeros_like(total_ref)
+
+    def one(peer, carry):
+        block = arrived_ref[peer]
+        base, weights = stencil(block[3 * rows : 6 * rows])
+        for k in range(rows):
+            at = slice(k * LANES, (k + 1) * LANES)
+            along_x = node_weights(size_x, base, weights, k)
+            along_y = node_weights(size_y, base, weights, rows + k)
+            high, low = split_two(node_weights(size_z, base, weights, 2 * rows + k))
+            right_ref[:size_z, at] = high
+            right_ref[size_z:, at] = low
+            for dimension in range(3):
+                scaled = along_x * block[dimension * rows + k : dimension * rows + k + 1, :]
+                for x in range(size_x):
+                    first = (dimension * size_x + x) * size_y
+                    high, low = split_two(along_y * scaled[x : x + 1, :])
+                    left_ref[first : first + size_y, at] = high
+                    left_ref[height + first : height + first + size_y, at] = low
+        total_ref[...] += lax.dot_general(
+            left_ref[...], right_ref[...], NT, preferred_element_type=jnp.float32
+        )
+        return carry
+
+    lax.fori_loop(0, arrived_ref.shape[0], one, 0)
+    field_ref[...] = (total_ref[height:, size_z:] + total_ref[height:, :size_z]) + (
+        total_ref[:height, size_z:] + total_ref[:height, :size_z]
+    )
+
+
+def spread(arrived, sizes, rows):
+    height = 3 * sizes[0] * sizes[1]
+    return pl.pallas_call(
+        lambda *refs: spread_kernel(sizes, rows, *refs),
+        out_shape=jax.ShapeDtypeStruct((height, sizes[2]), jnp.float32),
+        scratch_shapes=[
+            pltpu.VMEM((2 * height, rows * LANES), jnp.bfloat16),
+            pltpu.VMEM((2 * sizes[2], rows * LANES), jnp.bfloat16),
+            pltpu.VMEM((2 * height, 2 * sizes[2]), jnp.float32),
+        ],
+        compiler_params=pltpu.CompilerParams(vmem_limit_bytes=VMEM_LIMIT),
+        name="spread",
+    )(arrived)
+
+
+def sample_kernel(sizes, rows, arrived_ref, velocity_ref, sampled_ref, left_ref, right_ref, part_ref):
+    size_x, size_y, size_z = sizes
+    high, low = split_two(velocity_ref[...])
+    left_ref[:, :size_z] = high
+    left_ref[:, size_z : 2 * size_z] = low
+    left_ref[:, 2 * size_z :] = high
+
+    def one(peer, carry):
+        base, weights = stencil(arrived_ref[peer, 3 * rows : 6 * rows, :])
+        for k in range(rows):
+            at = slice(k * LANES, (k + 1) * LANES)
+            high, low = split_two(node_weights(size_z, base, weights, 2 * rows + k))
+            right_ref[:size_z, at] = high
+            right_ref[size_z : 2 * size_z, at] = high
+            right_ref[2 * size_z :, at] = low
+        part_ref[...] = lax.dot_general(
+            left_ref[...], right_ref[...], NN, preferred_element_type=jnp.float32
+        )
+        for k in range(rows):
+            at = slice(k * LANES, (k + 1) * LANES)
+            along_x = node_weights(size_x, base, weights, k)
+            along_y = node_weights(size_y, base, weights, rows + k)
+            for dimension in range(3):
+                total = jnp.zeros((size_y, LANES), jnp.float32)
+                for x in range(size_x):
+                    first = (dimension * size_x + x) * size_y
+                    total = total + along_x[x : x + 1, :] * part_ref[first : first + size_y, at]
+                across = jnp.sum(total * along_y, axis=0, keepdims=True)
+                sampled_ref[peer, dimension * rows + k : dimension * rows + k + 1, :] = (
+                    across / VELOCITY_UNIT
+                )
+        return carry
+
+    lax.fori_loop(0, arrived_ref.shape[0], one, 0)
+
+
+def sample(arrived, velocity, sizes, rows):
+    height = 3 * sizes[0] * sizes[1]
+    peers = arrived.shape[0]
+    return pl.pallas_call(
+        lambda *refs: sample_kernel(sizes, rows, *refs),
+        out_shape=jax.ShapeDtypeStruct((peers, 3 * rows, LANES), jnp.float32),
+        scratch_shapes=[
+            pltpu.VMEM((height, 3 * sizes[2]), jnp.bfloat16),
+            pltpu.VMEM((3 * sizes[2], rows * LANES), jnp.bfloat16),
+            pltpu.VMEM((height, rows * LANES), jnp.float32),
+        ],
+        compiler_params=pltpu.CompilerParams(vmem_limit_bytes=VMEM_LIMIT),
+        name="sample",
+    )(arrived, velocity)
+
+
+def collect_kernel(peers, rows, returned_ref, slot_ref, result_ref, table_ref, left_ref):
+    height = left_ref.shape[0] // 3
+    markers = result_ref.shape[1]
+    table_ref[...] = jnp.zeros_like(table_ref)
+    for row in range(3):
+        for peer in range(peers):
+            first = row * height + peer * rows
+            table_ref[first : first + rows, :] = returned_ref[peer, row * rows : (row + 1) * rows, :]
+    high, low = split_two(table_ref[...])
+    left_ref[:, :LANES] = high
+    left_ref[:, LANES:] = low
+
+    def one(chunk, width):
+        low_mask = iota((LANES, LANES), 0) == slot_ref[1, pl.ds(chunk, 1), :]
+        onehot = low_mask.astype(jnp.float32).astype(jnp.bfloat16)
+        found = lax.dot_general(
+            left_ref[...],
+            jnp.concatenate([onehot, onehot], axis=0),
+            NN,
+            preferred_element_type=jnp.float32,
+        )
+        high_mask = iota((height, LANES), 0) == slot_ref[0, pl.ds(chunk, 1), :]
+        values = jnp.concatenate(
+            [
+                jnp.sum(
+                    jnp.where(high_mask, found[row * height : (row + 1) * height], 0.0),
+                    axis=0,
+                    keepdims=True,
+                )
+                for row in range(3)
+            ],
+            axis=0,
+        )
+        if width == LANES:
+            result_ref[:, pl.ds(pl.multiple_of(chunk * LANES, LANES), LANES)] = values
+        else:
+            result_ref[:, markers - width :] = values[:, :width]
+
+    whole = markers // LANES
+
+    def step(chunk, carry):
+        one(chunk, LANES)
+        return carry
+
+    lax.fori_loop(0, whole, step, 0, unroll=4)
+    if markers % LANES:
+        one(whole, markers % LANES)
+
+
+def collect(returned, slots, markers, peers, rows):
+    height = -(-peers * rows // 16) * 16
+    return pl.pallas_call(
+        lambda *refs: collect_kernel(peers, rows, *refs),
+        out_shape=jax.ShapeDtypeStruct((3, markers), jnp.float32),
+        scratch_shapes=[
+            pltpu.VMEM((3 * height, LANES), jnp.float32),
+            pltpu.VMEM((3 * height, 2 * LANES), jnp.bfloat16),
+        ],
+        compiler_params=pltpu.CompilerParams(vmem_limit_bytes=VMEM_LIMIT),
+        name="collect",
+    )(returned, slots)
 
 
 def moving_rows(dimension):
@@ -135,35 +395,17 @@
     peer_count = lax.axis_size(("gz", "gy"))
     markers = displacement.shape[1]
     capacity = max(2, (2 * markers + peer_count - 1) // peer_count)
+    rows = -(-capacity // LANES)
+    chunks = -(-markers // LANES)
+    spare = chunks * LANES - markers
+    sizes = (size_x, size_y, size_z)
     forces = marker_forces(displacement, stiffness)
     position = base_node.astype(jnp.float32) + offset
-    target = destination[:, 0]
-    onehot = (target[:, None] == jnp.arange(peer_count, dtype=jnp.int32)[None, :]).astype(jnp.int32)
-    rank_in_peer = jnp.sum(jnp.cumsum(onehot, axis=0) * onehot, axis=1) - 1
-    slot_index = target * capacity + rank_in_peer
-    payload = jnp.concatenate([forces, position], axis=0)
-    outgoing = jnp.zeros((6, peer_count * capacity), jnp.float32).at[:, slot_index].set(payload)
-    arrived = lax.all_to_all(outgoing, ("gz", "gy"), split_axis=1, concat_axis=1, tiled=True)
-    slot_total = arrived.shape[1]
-    weight_x = axis_weights(size_x, arrived[3])
-    weight_y = axis_weights(size_y, arrived[4])
-    weight_z = axis_weights(size_z, arrived[5])
-    carried = arrived[0:3]
-
-    def spread_plane(plane_weight):
-        blended = (
-            carried[:, None, :] * plane_weight[None, None, :] * weight_y[None, :, :]
-        ).reshape(3 * size_y, slot_total)
-        return lax.dot_general(
-            blended,
-            weight_z,
-            (((1,), (1,)), ((), ())),
-            precision=lax.Precision.HIGHEST,
-            preferred_element_type=jnp.float32,
-        )
-
-    planes = lax.map(spread_plane, weight_x)
-    force_field = jnp.transpose(planes.reshape(size_x, 3, size_y, size_z), (1, 0, 2, 3))
+    target = jnp.pad(destination[:, 0], (0, spare), constant_values=-1).reshape(chunks, LANES)
+    payload = jnp.pad(jnp.concatenate([forces, position], axis=0), ((0, 0), (0, spare)))
+    outgoing, slots = route(target, payload, peer_count, rows)
+    arrived = lax.all_to_all(outgoing, ("gz", "gy"), split_axis=0, concat_axis=0, tiled=True)
+    force_field = spread(arrived, sizes, rows).reshape(3, size_x, size_y, size_z)
     post = collide(populations, force_field)
     moving = moving_rows(0)
     padded = padded_2(jnp.stack([post[index] for index in moving]), (("gx", 1),), 1)
@@ -174,26 +416,10 @@
     moving = moving_rows(2)
     padded = padded_2(jnp.stack([post[index] for index in moving]), (("gz", 3),), 1)
     new_populations = shift_along(post, padded, moving, 2, size_z)
-    velocity_planes = jnp.transpose(fluid_velocity(new_populations), (1, 0, 2, 3)).reshape(
-        size_x, 3 * size_y, size_z
-    )
-
-    def sample_plane(total, inputs):
-        plane, plane_weight = inputs
-        partial_value = jnp.dot(
-            plane, weight_z, precision=lax.Precision.HIGHEST, preferred_element_type=jnp.float32
-        )
-        across = jnp.sum(
-            partial_value.reshape(3, size_y, slot_total) * weight_y[None, :, :], axis=1
-        )
-        return (total + across * plane_weight[None, :], None)
-
-    sampled, unused = lax.scan(
-        sample_plane, jnp.zeros((3, slot_total), jnp.float32), (velocity_planes, weight_x)
-    )
-    sampled = sampled / VELOCITY_UNIT
-    returned = lax.all_to_all(sampled, ("gz", "gy"), split_axis=1, concat_axis=1, tiled=True)
-    marker_velocity = returned[:, slot_index]
+    velocity = fluid_velocity(new_populations).reshape(3 * size_x * size_y, size_z)
+    sampled = sample(arrived, velocity, sizes, rows)
+    returned = lax.all_to_all(sampled, ("gz", "gy"), split_axis=0, concat_axis=0, tiled=True)
+    marker_velocity = collect(returned, slots, markers, peer_count, rows)
     return (new_populations, marker_velocity)
 
 

time: 563 us -> 100 us (0.18)
  matrix products: 401 us -> 0 us
  local copies, waits for them, and re-layouts: 64.7 us -> 15.7 us
  other arithmetic: 51 us -> 7.51 us
  Pallas kernels: 0 us -> 34.7 us
  waiting for transfers between devices: 28.3 us -> 21.6 us
    dot_general x16 -> x0, matrix products: 401 us -> none  [the longest x8 215 us: sample_plane(): jnp.dot(plane, weight_z, precision=lax.Precision.HIGHEST, preferred_eleme...]
    select_n x18 -> x0, other arithmetic: 38.2 us -> none  [the longest x17 38.1 us: kernel(): jnp.where(jnp.abs(distance) < 2.0, 0.25 * (1.0 + jnp.cos(0.5 * math.pi *...]
    pallas_call x0 -> x4, Pallas kernels: none -> 34.7 us  [the longest x1 12.1 us: spread(): pl.pallas_call(lambda *refs: spread_kernel(sizes, rows, *refs), out_shape...]
    scatter x2 -> x0, local copies, waits for them, and re-layouts: 26.8 us -> none  [shards(): jnp.zeros((6, peer_count * capacity), jnp.float32).at[:, slot_index]]
    gather x1 -> x0, local copies, waits for them, and re-layouts: 11.1 us -> none  [shards(): marker_velocity = returned[:, slot_index]]
    ppermute x3, waiting for transfers between devices: 8.22 us -> 2.48 us  [padded_2(): before = lax.ppermute(last, axis, up)]
  transfers between devices with their start and end apart: 8 -> 8, of which waited for: 7 -> 7; matrix products, arithmetic and copies ran while one was open for 0% -> 5% of each run, Pallas kernels for 0% -> 0%
where the time goes in v1:
time: 100 us; the launch traced here: 99.3 us
  Pallas kernels  34.7 us (35%)
  waiting for transfers between devices  21.6 us (22%)
  starting transfers between devices  18.8 us (19%)
  local copies, waits for them, and re-layouts  15.7 us (16%)
  other arithmetic  7.51 us (8%)
  between operations  1.05 us (1%)
    pallas_call x1, Pallas kernels, spread(): pl.pallas_call(lambda *refs: spread_kernel(sizes, rows, *refs), out_shape...  12.1 us
    pallas_call x1, Pallas kernels, route(): pl.pallas_call(lambda *refs: route_kernel(peers, rows, *refs), out_shape=...  9.61 us
    all_to_all x1, waiting for transfers between devices, shards(): lax.all_to_all(outgoing, ('gz', 'gy'), split_axis=0, concat_axis=0, tiled...  9.53 us
    pallas_call x1, Pallas kernels, sample(): pl.pallas_call(lambda *refs: sample_kernel(sizes, rows, *refs), out_shape...  8.75 us
    all_to_all x1, waiting for transfers between devices, shards(): lax.all_to_all(sampled, ('gz', 'gy'), split_axis=0, concat_axis=0, tiled=...  7.46 us
    all_to_all x1, starting transfers between devices, shards(): lax.all_to_all(outgoing, ('gz', 'gy'), split_axis=0, concat_axis=0, tiled...  7.25 us
    ppermute x3, starting transfers between devices, padded_2(): after = lax.ppermute(initial, axis, down)  5.5 us
    all_to_all x1, starting transfers between devices, shards(): lax.all_to_all(sampled, ('gz', 'gy'), split_axis=0, concat_axis=0, tiled=...  5.05 us
  transfers between devices with their start and end apart: 8, of which 7 were waited for; matrix products, arithmetic and copies ran while one was open for 5% of the time, Pallas kernels for 0%

profile of v1, /device:TPU:0, one launch (start us, length us, event | category | flops | bytes accessed | tf_op | source)
XLA Modules:
  0.0 99.3 jit_solution(17916273563739843323)
XLA Ops:
  0.6 0.8 mul.1658
  2.4 1.0 %reshape.248 = f32[3,8,642]{2,1,0:T(8,128)S(1)} reshape(f32[3,5136]{1,0:T(4,128)} %param.7) | data formatting | bytes 123264 | tf_op jit(solution)/shard_map/reshape | solution.py:53
  3.7 1.0 %convert_add_fusion = (f32[3,5136]{1,0:T(4,128)S(1)}, f32[3,5136]{1,0:T(4,128)S(1)}) fusion(f32[3,5136]{1,0:T(4,128)} %param.10, s32[3,5136]{1,0:T(4,128)} %param.9, f32[3,5136]{1,0:T(4,128)} %param.7, f32[3,5136]{1,0:T(4,128)S(1)} %sub.390, f32[5136]{0:T(1024)S(1)} %mul.1659), kind=kLoop, calls=%fused_computation.89 | loop fusion | flops 61632 | bytes 390336 | tf_op jit(solution)/shard_map/add | solution.py:403
  4.8 9.6 %route.1 = (f32[8,66,128]{2,1,0:T(8,128)}, s32[2,41,128]{2,1,0:T(8,128)S(1)}) custom-call(s32[41,128]{1,0:T(8,128)S(1)} %pad_bitcast_fusion.refs_0_, f32[6,5248]{1,0:T(8,128)S(1)} %select_maximum_fusion.refs_1_), custom_call_target="tpu_custom_call" | custom-call | tf_op jit(solution)/shard_map/route/pallas_call | solution.py:185
  14.4 7.3 %all-to-all-start = ((f32[8,66,128]{2,1,0:T(8,128)}), f32[8,66,128]{2,1,0:T(8,128)S(1)}, u32[]{:S(2)}, u32[]{:S(2)}) async-start(f32[8,66,128]{2,1,0:T(8,128)} %get-tuple-element.4), calls=%async_computation | async-start | bytes 589824 | tf_op jit(solution)/shard_map/all_to_all | solution.py:407
  21.7 9.5 %all-to-all-done.refs_0_ = f32[8,66,128]{2,1,0:T(8,128)S(1)} async-done(((f32[8,66,128]{2,1,0:T(8,128)}), f32[8,66,128]{2,1,0:T(8,128)S(1)}, u32[]{:S(2)}, u32[]{:S(2)}) %all-to-all-start) | async-done | bytes 270368 | tf_op jit(solution)/shard_map/all_to_all | solution.py:407
  31.2 12.1 %spread.1 = f32[384,128]{1,0:T(8,128)S(1)} custom-call(f32[8,66,128]{2,1,0:T(8,128)S(1)} %all-to-all-done.refs_0_), custom_call_target="tpu_custom_call" | custom-call | tf_op jit(solution)/shard_map/spread/pallas_call | solution.py:251
  43.4 0.8 constant_dynamic-update-slice_fusion.29
  48.0 1.5 %collective-permute-start.3 = (f32[10,8,1,128]{3,1,2,0:T(8,128)S(1)}, f32[10,8,1,128]{3,1,2,0:T(8,128)S(1)}, u32[]{:S(2)}, u32[]{:S(2)}) collective-permute-start(f32[10,8,1,128]{3,1,2,0:T(8,128)S(1)} %bitcast.335), channel_id=1, source_target_pairs={{2,0},{0,2},{3,1},{1,3},{6,4},{4,6},{7,5},{5,7},{10,8},{8,10},{11,... | collective-permute-start | bytes 122888 | tf_op jit(solution)/shard_map/ppermute | solution.py:47
  50.1 1.9 %collective-permute-done.3 = f32[10,8,1,128]{3,1,2,0:T(8,128)S(1)} collective-permute-done((f32[10,8,1,128]{3,1,2,0:T(8,128)S(1)}, f32[10,8,1,128]{3,1,2,0:T(8,128)S(1)}, u32[]{:S(2)}, u32[]{:S(2)}) %collective-permute-start.3) | collective-permute-done | bytes 40992 | tf_op jit(solution)/shard_map/ppermute | solution.py:47
  52.1 1.4 %collective-permute-done.2 = f32[10,8,1,128]{3,1,2,0:T(8,128)S(1)} collective-permute-done((f32[10,8,1,128]{3,1,2,0:T(8,128)S(1)}, f32[10,8,1,128]{3,1,2,0:T(8,128)S(1)}, u32[]{:S(2)}, u32[]{:S(2)}) %collective-permute-start.2) | collective-permute-done | bytes 40992 | tf_op jit(solution)/shard_map/ppermute | solution.py:46
  53.6 0.8 slice_bitcast_fusion.19
  54.5 1.3 %fusion.149 = (f32[10,8,16,1]{3,2,1,0:T(8,128)}, f32[10,8,16,1]{3,2,1,0:T(8,128)}) fusion(f32[10,8,16,128]{3,2,1,0:T(8,128)S(1)} %constant_dynamic-update-slice_fusion.20), kind=kLoop, calls=%fused_computation.276 | loop fusion | bytes 20480 | tf_op jit(solution)/shard_map/slice | solution.py:44
  55.8 2.2 %copy.116 = f32[10,8,16,1]{2,1,3,0:T(8,128)} copy(f32[10,8,16,1]{3,2,1,0:T(8,128)} %get-tuple-element.46) | data formatting | bytes 10240 | tf_op jit(solution)/shard_map/slice | solution.py:44
  58.3 2.2 %copy.117 = f32[10,8,16,1]{2,1,3,0:T(8,128)} copy(f32[10,8,16,1]{3,2,1,0:T(8,128)} %get-tuple-element.47) | data formatting | bytes 10240 | tf_op jit(solution)/shard_map/slice | solution.py:45
  60.5 3.5 %collective-permute-start.5 = (f32[10,8,16,1]{2,1,3,0:T(8,128)}, f32[10,8,16,1]{2,1,3,0:T(8,128)}, u32[]{:S(2)}, u32[]{:S(2)}) collective-permute-start(f32[10,8,16,1]{2,1,3,0:T(8,128)} %copy.117), channel_id=1, source_target_pairs={{4,0},{8,4},{12,8},{0,12},{5,1},{9,5},{13,9},{1,13},{6,2},{10,6},{... | collective-permute-start | bytes 15368 | tf_op jit(solution)/shard_map/ppermute | solution.py:47
  64.4 2.2 %copy.118 = f32[10,8,16,1]{3,2,1,0:T(8,128)} copy(f32[10,8,16,1]{2,1,3,0:T(8,128)} %collective-permute-done.4) | data formatting | bytes 10240 | tf_op jit(solution)/shard_map/ppermute | solution.py:46
  66.5 2.2 %copy.119 = f32[10,8,16,1]{3,2,1,0:T(8,128)} copy(f32[10,8,16,1]{2,1,3,0:T(8,128)} %collective-permute-done.5) | data formatting | bytes 10240 | tf_op jit(solution)/shard_map/ppermute | solution.py:47
  68.7 1.9 %pad_maximum_fusion = f32[10,8,16,130]{3,2,1,0:T(8,128)S(1)} fusion(f32[10,8,16,1]{3,2,1,0:T(8,128)} %copy.119, f32[10,8,16,128]{3,2,1,0:T(8,128)S(1)} %constant_dynamic-update-slice_fusion.20, f32[10,8,16,1]{3,2,1,0:T(8,128)} %copy.118), kind=kLoop, calls=%fused_computation | loop fusion | flops 332800 | bytes 1331200 | tf_op jit(solution)/shard_map/concatenate | solution.py:48
  72.2 1.0 %copy-done.8 = f32[19,8,16,128]{3,2,1,0:T(8,128)S(1)} copy-done((f32[19,8,16,128]{3,2,1,0:T(8,128)S(1)}, f32[19,8,16,128]{3,2,1,0:T(8,128)}, u32[]{:S(2)}) %copy-start.8) | copy-done | bytes 1245208
  73.7 8.8 %sample.1 = f32[8,33,128]{2,1,0:T(8,128)} custom-call(f32[8,66,128]{2,1,0:T(8,128)S(1)} %all-to-all-done.refs_0_, f32[384,128]{1,0:T(8,128)S(1)} %bitcast.285), custom_call_target="tpu_custom_call" | custom-call | tf_op jit(solution)/shard_map/sample/pallas_call | solution.py:303
  82.4 5.1 %all-to-all-start.1 = ((f32[8,33,128]{2,1,0:T(8,128)}), f32[8,33,128]{2,1,0:T(8,128)S(1)}, u32[]{:S(2)}, u32[]{:S(2)}) async-start(f32[8,33,128]{2,1,0:T(8,128)} %sample.1), calls=%async_computation.1 | async-start | bytes 327680 | tf_op jit(solution)/shard_map/all_to_all | solution.py:421
  87.6 7.5 %all-to-all-done.1.refs_0_ = f32[8,33,128]{2,1,0:T(8,128)S(1)} async-done(((f32[8,33,128]{2,1,0:T(8,128)}), f32[8,33,128]{2,1,0:T(8,128)S(1)}, u32[]{:S(2)}, u32[]{:S(2)}) %all-to-all-start.1) | async-done | bytes 135200 | tf_op jit(solution)/shard_map/all_to_all | solution.py:421
  95.1 4.2 %collect.1 = f32[3,5136]{1,0:T(4,128)} custom-call(f32[8,33,128]{2,1,0:T(8,128)S(1)} %all-to-all-done.1.refs_0_, s32[2,41,128]{2,1,0:T(8,128)S(1)} %get-tuple-element.5.refs_1_), custom_call_target="tpu_custom_call" | custom-call | tf_op jit(solution)/shard_map/collect/pallas_call | solution.py:367
  (89 shorter events, 8.4 us)
Async XLA Ops:
  0.6 21.0 %copy-start = (f32[19,8,16,128]{3,2,1,0:T(8,128)S(1)}, f32[19,8,16,128]{3,2,1,0:T(8,128)}, u32[]{:S(2)}) copy-start(f32[19,8,16,128]{3,2,1,0:T(8,128)} %param.6) | copy-start | bytes 3735556
  14.4 16.9 %all-to-all-start = ((f32[8,66,128]{2,1,0:T(8,128)}), f32[8,66,128]{2,1,0:T(8,128)S(1)}, u32[]{:S(2)}, u32[]{:S(2)}) async-start(f32[8,66,128]{2,1,0:T(8,128)} %get-tuple-element.4), calls=%async_computation | async-start | bytes 589824 | tf_op jit(solution)/shard_map/all_to_all | solution.py:407
  45.3 1.3 %collective-permute-start = (f32[10,1,16,128]{3,2,1,0:T(8,128)S(1)}, f32[10,1,16,128]{3,2,1,0:T(8,128)S(1)}, u32[]{:S(2)}, u32[]{:S(2)}) collective-permute-start(f32[10,1,16,128]{3,2,1,0:T(8,128)S(1)} %get-tuple-element.51), channel_id=1, source_target_pairs={{0,1},{1,0},{2,3},{3,2},{4,5},{5,4},{6,7},{7,6},{8,9},{9,8},{10,11... | collective-permute-start | bytes 245768 | tf_op jit(solution)/shard_map/ppermute | solution.py:46
  45.4 1.4 %collective-permute-start.1 = (f32[10,1,16,128]{3,2,1,0:T(8,128)S(1)}, f32[10,1,16,128]{3,2,1,0:T(8,128)S(1)}, u32[]{:S(2)}, u32[]{:S(2)}) collective-permute-start(f32[10,1,16,128]{3,2,1,0:T(8,128)S(1)} %get-tuple-element.50), channel_id=1, source_target_pairs={{1,0},{0,1},{3,2},{2,3},{5,4},{4,5},{7,6},{6,7},{9,8},{8,9},{11,10... | collective-permute-start | bytes 245768 | tf_op jit(solution)/shard_map/ppermute | solution.py:47
  48.0 4.1 %collective-permute-start.3 = (f32[10,8,1,128]{3,1,2,0:T(8,128)S(1)}, f32[10,8,1,128]{3,1,2,0:T(8,128)S(1)}, u32[]{:S(2)}, u32[]{:S(2)}) collective-permute-start(f32[10,8,1,128]{3,1,2,0:T(8,128)S(1)} %bitcast.335), channel_id=1, source_target_pairs={{2,0},{0,2},{3,1},{1,3},{6,4},{4,6},{7,5},{5,7},{10,8},{8,10},{11,... | collective-permute-start | bytes 122888 | tf_op jit(solution)/shard_map/ppermute | solution.py:47
  49.5 4.0 %collective-permute-start.2 = (f32[10,8,1,128]{3,1,2,0:T(8,128)S(1)}, f32[10,8,1,128]{3,1,2,0:T(8,128)S(1)}, u32[]{:S(2)}, u32[]{:S(2)}) collective-permute-start(f32[10,8,1,128]{3,1,2,0:T(8,128)S(1)} %bitcast.334), channel_id=1, source_target_pairs={{0,2},{2,0},{1,3},{3,1},{4,6},{6,4},{5,7},{7,5},{8,10},{10,8},{9,1... | collective-permute-start | bytes 122888 | tf_op jit(solution)/shard_map/ppermute | solution.py:46
  58.0 6.4 %collective-permute-start.4 = (f32[10,8,16,1]{2,1,3,0:T(8,128)}, f32[10,8,16,1]{2,1,3,0:T(8,128)}, u32[]{:S(2)}, u32[]{:S(2)}) collective-permute-start(f32[10,8,16,1]{2,1,3,0:T(8,128)} %copy.116), channel_id=1, source_target_pairs={{0,4},{4,8},{8,12},{12,0},{1,5},{5,9},{9,13},{13,1},{2,6},{6,10},{... | collective-permute-start | bytes 15368 | tf_op jit(solution)/shard_map/ppermute | solution.py:46
  60.5 6.0 %collective-permute-start.5 = (f32[10,8,16,1]{2,1,3,0:T(8,128)}, f32[10,8,16,1]{2,1,3,0:T(8,128)}, u32[]{:S(2)}, u32[]{:S(2)}) collective-permute-start(f32[10,8,16,1]{2,1,3,0:T(8,128)} %copy.117), channel_id=1, source_target_pairs={{4,0},{8,4},{12,8},{0,12},{5,1},{9,5},{13,9},{1,13},{6,2},{10,6},{... | collective-permute-start | bytes 15368 | tf_op jit(solution)/shard_map/ppermute | solution.py:47
  70.6 0.9 copy-start.1
  70.6 0.9 copy-start.2
  70.6 1.0 copy-start.3
  70.6 1.0 %copy-start.4 = (f32[8,18,128]{2,1,0:T(8,128)S(1)}, f32[8,18,128]{2,1,0:T(8,128)}, u32[]{:S(2)}) copy-start(f32[8,18,128]{2,1,0:T(8,128)} %get-tuple-element.36) | copy-start | bytes 221188
  70.6 1.0 %copy-start.5 = (f32[1,8,16,128]{3,2,1,0:T(8,128)S(1)}, f32[1,8,16,128]{3,2,1,0:T(8,128)}, u32[]{:S(2)}) copy-start(f32[1,8,16,128]{3,2,1,0:T(8,128)} %get-tuple-element.14) | copy-start | bytes 196612
  70.6 1.0 %copy-start.6 = (f32[1,8,16,128]{3,2,1,0:T(8,128)S(1)}, f32[1,8,16,128]{3,2,1,0:T(8,128)}, u32[]{:S(2)}) copy-start(f32[1,8,16,128]{3,2,1,0:T(8,128)} %get-tuple-element.16) | copy-start | bytes 196612
  70.6 1.0 %copy-start.7 = (f32[1,8,16,128]{3,2,1,0:T(8,128)S(1)}, f32[1,8,16,128]{3,2,1,0:T(8,128)}, u32[]{:S(2)}) copy-start(f32[1,8,16,128]{3,2,1,0:T(8,128)} %get-tuple-element.18) | copy-start | bytes 196612
  71.9 1.3 %copy-start.8 = (f32[19,8,16,128]{3,2,1,0:T(8,128)S(1)}, f32[19,8,16,128]{3,2,1,0:T(8,128)}, u32[]{:S(2)}) copy-start(f32[19,8,16,128]{3,2,1,0:T(8,128)} %get-tuple-element.20) | copy-start | bytes 3735556
  82.4 12.6 %all-to-all-start.1 = ((f32[8,33,128]{2,1,0:T(8,128)}), f32[8,33,128]{2,1,0:T(8,128)S(1)}, u32[]{:S(2)}, u32[]{:S(2)}) async-start(f32[8,33,128]{2,1,0:T(8,128)} %sample.1), calls=%async_computation.1 | async-start | bytes 327680 | tf_op jit(solution)/shard_map/all_to_all | solution.py:421
  87.6 11.7 %copy-start.9 = (f32[19,8,16,128]{3,2,1,0:T(8,128)}, f32[19,8,16,128]{3,2,1,0:T(8,128)S(1)}, u32[]{:S(2)}) copy-start(f32[19,8,16,128]{3,2,1,0:T(8,128)S(1)} %constant_dynamic-update-slice_fusion.30) | copy-start | bytes 3735556

commit v2 on v1

--- a/solution.py
+++ b/solution.py
@@ -124,7 +124,47 @@
     return high, (value - high.astype(jnp.float32)).astype(jnp.bfloat16)
 
 
-def route_kernel(peers, rows, target_ref, payload_ref, sent_ref, slot_ref, left_ref, right_ref):
+MESH = pl.DeviceIdType.MESH
+PEERS = ("gz", "gy")
+
+
+def peer_device(peer):
+    across = lax.axis_size("gy")
+    return {"gz": lax.div(peer, across), "gy": lax.rem(peer, across)}
+
+
+def exchange(peers, sent_ref, received_ref, send_sem, recv_sem):
+    me = lax.axis_index(PEERS)
+
+    def copy(step):
+        peer = lax.rem(me + step, peers)
+        return pltpu.make_async_remote_copy(
+            src_ref=sent_ref.at[peer],
+            dst_ref=received_ref.at[me],
+            send_sem=send_sem.at[step],
+            recv_sem=recv_sem.at[step],
+            device_id=peer_device(peer),
+            device_id_type=MESH,
+        )
+
+    return copy
+
+
+def greet_peers(peers):
+    me = lax.axis_index(PEERS)
+    barrier = pltpu.get_barrier_semaphore()
+
+    def greet(step, carry):
+        pl.semaphore_signal(
+            barrier, inc=1, device_id=peer_device(lax.rem(me + step, peers)), device_id_type=MESH
+        )
+        return carry
+
+    lax.fori_loop(1, peers, greet, 0)
+    return barrier
+
+
+def route_part(peers, rows, target_ref, payload_ref, sent_ref, slot_ref, left_ref, right_ref):
     chunks = target_ref.shape[0]
     target = target_ref[...]
     bf16 = jnp.bfloat16
@@ -179,24 +219,6 @@
             sent_ref[peer, row * rows : (row + 1) * rows, :] = total[peer * rows : (peer + 1) * rows]
 
 
-def route(target, payload, peers, rows):
-    chunks = target.shape[0]
-    height = -(-peers * rows // 16) * 16
-    return pl.pallas_call(
-        lambda *refs: route_kernel(peers, rows, *refs),
-        out_shape=(
-            jax.ShapeDtypeStruct((peers, 6 * rows, LANES), jnp.float32),
-            jax.ShapeDtypeStruct((2, chunks, LANES), jnp.int32),
-        ),
-        scratch_shapes=[
-            pltpu.VMEM((15 * height, chunks * LANES), jnp.bfloat16),
-            pltpu.VMEM((LANES, chunks * LANES), jnp.bfloat16),
-        ],
-        compiler_params=pltpu.CompilerParams(vmem_limit_bytes=VMEM_LIMIT),
-        name="route",
-    )(target, payload)
-
-
 def stencil(position):
     base = jnp.floor(position)
     angle = (0.5 * math.pi) * (position - base)
@@ -213,107 +235,131 @@
     return result
 
 
-def spread_kernel(sizes, rows, arrived_ref, field_ref, left_ref, right_ref, total_ref):
+def spread_part(sizes, rows, block, left_ref, right_ref, total_ref):
     size_x, size_y, size_z = sizes
     height = 3 * size_x * size_y
+    base, weights = stencil(block[3 * rows : 6 * rows])
+    for k in range(rows):
+        at = slice(k * LANES, (k + 1) * LANES)
+        along_x = node_weights(size_x, base, weights, k)
+        along_y = node_weights(size_y, base, weights, rows + k)
+        high, low = split_two(node_weights(size_z, base, weights, 2 * rows + k))
+        right_ref[:size_z, at] = high
+        right_ref[size_z:, at] = low
+        for dimension in range(3):
+            scaled = along_x * block[dimension * rows + k : dimension * rows + k + 1, :]
+            for x in range(size_x):
+                first = (dimension * size_x + x) * size_y
+                high, low = split_two(along_y * scaled[x : x + 1, :])
+                left_ref[first : first + size_y, at] = high
+                left_ref[height + first : height + first + size_y, at] = low
+    total_ref[...] += lax.dot_general(
+        left_ref[...], right_ref[...], NT, preferred_element_type=jnp.float32
+    )
+
+
+def outward_kernel(
+    peers, rows, sizes, target_ref, payload_ref, field_ref, slot_ref, position_ref,
+    route_left, route_right, sent_ref, arrived_ref, left_ref, right_ref, total_ref,
+    send_sem, recv_sem,
+):
+    me = lax.axis_index(PEERS)
+    size_z = sizes[2]
+    height = 3 * sizes[0] * sizes[1]
+    barrier = greet_peers(peers)
+    route_part(peers, rows, target_ref, payload_ref, sent_ref, slot_ref, route_left, route_right)
+    pl.semaphore_wait(barrier, peers - 1)
+    copy = exchange(peers, sent_ref, arrived_ref, send_sem, recv_sem)
+
+    def send(step, carry):
+        copy(step).start()
+        return carry
+
+    lax.fori_loop(1, peers, send, 0)
     total_ref[...] = jnp.zeros_like(total_ref)
 
-    def one(peer, carry):
-        block = arrived_ref[peer]
-        base, weights = stencil(block[3 * rows : 6 * rows])
-        for k in range(rows):
-            at = slice(k * LANES, (k + 1) * LANES)
-            along_x = node_weights(size_x, base, weights, k)
-            along_y = node_weights(size_y, base, weights, rows + k)
-            high, low = split_two(node_weights(size_z, base, weights, 2 * rows + k))
-            right_ref[:size_z, at] = high
-            right_ref[size_z:, at] = low
-            for dimension in range(3):
-                scaled = along_x * block[dimension * rows + k : dimension * rows + k + 1, :]
-                for x in range(size_x):
-                    first = (dimension * size_x + x) * size_y
-                    high, low = split_two(along_y * scaled[x : x + 1, :])
-                    left_ref[first : first + size_y, at] = high
-                    left_ref[height + first : height + first + size_y, at] = low
-        total_ref[...] += lax.dot_general(
-            left_ref[...], right_ref[...], NT, preferred_element_type=jnp.float32
-        )
-        return carry
-
-    lax.fori_loop(0, arrived_ref.shape[0], one, 0)
+    def add(source, block):
+        position_ref[source] = block[3 * rows : 6 * rows]
+        spread_part(sizes, rows, block, left_ref, right_ref, total_ref)
+
+    add(me, sent_ref[me])
+
+    def one(step, carry):
+        copy(step).wait_recv()
+        source = lax.rem(me + peers - step, peers)
+        add(source, arrived_ref[source])
+        return carry
+
+    lax.fori_loop(1, peers, one, 0)
     field_ref[...] = (total_ref[height:, size_z:] + total_ref[height:, :size_z]) + (
         total_ref[:height, size_z:] + total_ref[:height, :size_z]
     )
 
-
-def spread(arrived, sizes, rows):
+    def finish(step, carry):
+        copy(step).wait_send()
+        return carry
+
+    lax.fori_loop(1, peers, finish, 0)
+
+
+def outward(target, payload, peers, rows, sizes):
+    chunks = target.shape[0]
+    slots_high = -(-peers * rows // 16) * 16
     height = 3 * sizes[0] * sizes[1]
     return pl.pallas_call(
-        lambda *refs: spread_kernel(sizes, rows, *refs),
-        out_shape=jax.ShapeDtypeStruct((height, sizes[2]), jnp.float32),
+        lambda *refs: outward_kernel(peers, rows, sizes, *refs),
+        out_shape=(
+            jax.ShapeDtypeStruct((height, sizes[2]), jnp.float32),
+            jax.ShapeDtypeStruct((2, chunks, LANES), jnp.int32),
+            jax.ShapeDtypeStruct((peers, 3 * rows, LANES), jnp.float32),
+        ),
+        in_specs=[pl.BlockSpec(memory_space=pltpu.VMEM)] * 2,
+        out_specs=(pl.BlockSpec(memory_space=pltpu.VMEM),) * 3,
         scratch_shapes=[
+            pltpu.VMEM((15 * slots_high, chunks * LANES), jnp.bfloat16),
+            pltpu.VMEM((LANES, chunks * LANES), jnp.bfloat16),
+            pltpu.VMEM((peers, 6 * rows, LANES), jnp.float32),
+            pltpu.VMEM((peers, 6 * rows, LANES), jnp.float32),
             pltpu.VMEM((2 * height, rows * LANES), jnp.bfloat16),
             pltpu.VMEM((2 * sizes[2], rows * LANES), jnp.bfloat16),
             pltpu.VMEM((2 * height, 2 * sizes[2]), jnp.float32),
+            pltpu.SemaphoreType.DMA((peers,)),
+            pltpu.SemaphoreType.DMA((peers,)),
         ],
-        compiler_params=pltpu.CompilerParams(vmem_limit_bytes=VMEM_LIMIT),
-        name="spread",
-    )(arrived)
-
-
-def sample_kernel(sizes, rows, arrived_ref, velocity_ref, sampled_ref, left_ref, right_ref, part_ref):
+        compiler_params=pltpu.CompilerParams(
+            vmem_limit_bytes=VMEM_LIMIT, collective_id=0, has_side_effects=True
+        ),
+        name="outward",
+    )(target, payload)
+
+
+def sample_part(sizes, rows, position, left_ref, right_ref, part_ref):
     size_x, size_y, size_z = sizes
-    high, low = split_two(velocity_ref[...])
-    left_ref[:, :size_z] = high
-    left_ref[:, size_z : 2 * size_z] = low
-    left_ref[:, 2 * size_z :] = high
-
-    def one(peer, carry):
-        base, weights = stencil(arrived_ref[peer, 3 * rows : 6 * rows, :])
-        for k in range(rows):
-            at = slice(k * LANES, (k + 1) * LANES)
-            high, low = split_two(node_weights(size_z, base, weights, 2 * rows + k))
-            right_ref[:size_z, at] = high
-            right_ref[size_z : 2 * size_z, at] = high
-            right_ref[2 * size_z :, at] = low
-        part_ref[...] = lax.dot_general(
-            left_ref[...], right_ref[...], NN, preferred_element_type=jnp.float32
-        )
-        for k in range(rows):
-            at = slice(k * LANES, (k + 1) * LANES)
-            along_x = node_weights(size_x, base, weights, k)
-            along_y = node_weights(size_y, base, weights, rows + k)
-            for dimension in range(3):
-                total = jnp.zeros((size_y, LANES), jnp.float32)
-                for x in range(size_x):
-                    first = (dimension * size_x + x) * size_y
-                    total = total + along_x[x : x + 1, :] * part_ref[first : first + size_y, at]
-                across = jnp.sum(total * along_y, axis=0, keepdims=True)
-                sampled_ref[peer, dimension * rows + k : dimension * rows + k + 1, :] = (
-                    across / VELOCITY_UNIT
-                )
-        return carry
-
-    lax.fori_loop(0, arrived_ref.shape[0], one, 0)
-
-
-def sample(arrived, velocity, sizes, rows):
-    height = 3 * sizes[0] * sizes[1]
-    peers = arrived.shape[0]
-    return pl.pallas_call(
-        lambda *refs: sample_kernel(sizes, rows, *refs),
-        out_shape=jax.ShapeDtypeStruct((peers, 3 * rows, LANES), jnp.float32),
-        scratch_shapes=[
-            pltpu.VMEM((height, 3 * sizes[2]), jnp.bfloat16),
-            pltpu.VMEM((3 * sizes[2], rows * LANES), jnp.bfloat16),
-            pltpu.VMEM((height, rows * LANES), jnp.float32),
-        ],
-        compiler_params=pltpu.CompilerParams(vmem_limit_bytes=VMEM_LIMIT),
-        name="sample",
-    )(arrived, velocity)
-
-
-def collect_kernel(peers, rows, returned_ref, slot_ref, result_ref, table_ref, left_ref):
+    base, weights = stencil(position)
+    for k in range(rows):
+        at = slice(k * LANES, (k + 1) * LANES)
+        high, low = split_two(node_weights(size_z, base, weights, 2 * rows + k))
+        right_ref[:size_z, at] = high
+        right_ref[size_z : 2 * size_z, at] = high
+        right_ref[2 * size_z :, at] = low
+    part_ref[...] = lax.dot_general(
+        left_ref[...], right_ref[...], NN, preferred_element_type=jnp.float32
+    )
+    result = [[], [], []]
+    for k in range(rows):
+        at = slice(k * LANES, (k + 1) * LANES)
+        along_x = node_weights(size_x, base, weights, k)
+        along_y = node_weights(size_y, base, weights, rows + k)
+        for dimension in range(3):
+            total = jnp.zeros((size_y, LANES), jnp.float32)
+            for x in range(size_x):
+                first = (dimension * size_x + x) * size_y
+                total = total + along_x[x : x + 1, :] * part_ref[first : first + size_y, at]
+            result[dimension].append(jnp.sum(total * along_y, axis=0, keepdims=True))
+    return jnp.concatenate(result[0] + result[1] + result[2], axis=0) / VELOCITY_UNIT
+
+
+def collect_part(peers, rows, returned_ref, slot_ref, result_ref, table_ref, left_ref):
     height = left_ref.shape[0] // 3
     markers = result_ref.shape[1]
     table_ref[...] = jnp.zeros_like(table_ref)
@@ -325,7 +371,7 @@
     left_ref[:, :LANES] = high
     left_ref[:, LANES:] = low
 
-    def one(chunk, width):
+    def one(chunk):
         low_mask = iota((LANES, LANES), 0) == slot_ref[1, pl.ds(chunk, 1), :]
         onehot = low_mask.astype(jnp.float32).astype(jnp.bfloat16)
         found = lax.dot_general(
@@ -335,7 +381,7 @@
             preferred_element_type=jnp.float32,
         )
         high_mask = iota((height, LANES), 0) == slot_ref[0, pl.ds(chunk, 1), :]
-        values = jnp.concatenate(
+        return jnp.concatenate(
             [
                 jnp.sum(
                     jnp.where(high_mask, found[row * height : (row + 1) * height], 0.0),
@@ -346,34 +392,78 @@
             ],
             axis=0,
         )
-        if width == LANES:
-            result_ref[:, pl.ds(pl.multiple_of(chunk * LANES, LANES), LANES)] = values
-        else:
-            result_ref[:, markers - width :] = values[:, :width]
-
-    whole = markers // LANES
+
+    whole, rest = markers // LANES, markers % LANES
 
     def step(chunk, carry):
-        one(chunk, LANES)
+        result_ref[:, pl.ds(pl.multiple_of(chunk * LANES, LANES), LANES)] = one(chunk)
         return carry
 
     lax.fori_loop(0, whole, step, 0, unroll=4)
-    if markers % LANES:
-        one(whole, markers % LANES)
-
-
-def collect(returned, slots, markers, peers, rows):
-    height = -(-peers * rows // 16) * 16
+    if rest:
+        result_ref[:, markers - rest :] = one(whole)[:, :rest]
+
+
+def homeward_kernel(
+    peers, rows, sizes, position_ref, velocity_ref, slot_ref, result_ref,
+    sampled_ref, returned_ref, left_ref, right_ref, part_ref, table_ref, table_left,
+    send_sem, recv_sem,
+):
+    me = lax.axis_index(PEERS)
+    size_z = sizes[2]
+    barrier = greet_peers(peers)
+    high, low = split_two(velocity_ref[...])
+    left_ref[:, :size_z] = high
+    left_ref[:, size_z : 2 * size_z] = low
+    left_ref[:, 2 * size_z :] = high
+    pl.semaphore_wait(barrier, peers - 1)
+    copy = exchange(peers, sampled_ref, returned_ref, send_sem, recv_sem)
+
+    def one(step, carry):
+        peer = lax.rem(me + step, peers)
+        sampled_ref[peer] = sample_part(
+            sizes, rows, position_ref[peer], left_ref, right_ref, part_ref
+        )
+        copy(step).start()
+        return carry
+
+    lax.fori_loop(1, peers, one, 0)
+    returned_ref[me] = sample_part(sizes, rows, position_ref[me], left_ref, right_ref, part_ref)
+
+    def finish(step, carry):
+        copy(step).wait_recv()
+        copy(step).wait_send()
+        return carry
+
+    lax.fori_loop(1, peers, finish, 0)
+    collect_part(peers, rows, returned_ref, slot_ref, result_ref, table_ref, table_left)
+
+
+def homeward(position, velocity, slots, markers, rows, sizes):
+    peers = position.shape[0]
+    slots_high = -(-peers * rows // 16) * 16
+    height = 3 * sizes[0] * sizes[1]
     return pl.pallas_call(
-        lambda *refs: collect_kernel(peers, rows, *refs),
+        lambda *refs: homeward_kernel(peers, rows, sizes, *refs),
         out_shape=jax.ShapeDtypeStruct((3, markers), jnp.float32),
+        in_specs=[pl.BlockSpec(memory_space=pltpu.VMEM)] * 3,
+        out_specs=pl.BlockSpec(memory_space=pltpu.VMEM),
         scratch_shapes=[
-            pltpu.VMEM((3 * height, LANES), jnp.float32),
-            pltpu.VMEM((3 * height, 2 * LANES), jnp.bfloat16),
+            pltpu.VMEM((peers, 3 * rows, LANES), jnp.float32),
+            pltpu.VMEM((peers, 3 * rows, LANES), jnp.float32),
+            pltpu.VMEM((height, 3 * sizes[2]), jnp.bfloat16),
+            pltpu.VMEM((3 * sizes[2], rows * LANES), jnp.bfloat16),
+            pltpu.VMEM((height, rows * LANES), jnp.float32),
+            pltpu.VMEM((3 * slots_high, LANES), jnp.float32),
+            pltpu.VMEM((3 * slots_high, 2 * LANES), jnp.bfloat16),
+            pltpu.SemaphoreType.DMA((peers,)),
+            pltpu.SemaphoreType.DMA((peers,)),
         ],
-        compiler_params=pltpu.CompilerParams(vmem_limit_bytes=VMEM_LIMIT),
-        name="collect",
-    )(returned, slots)
+        compiler_params=pltpu.CompilerParams(
+            vmem_limit_bytes=VMEM_LIMIT, collective_id=1, has_side_effects=True
+        ),
+        name="homeward",
+    )(position, velocity, slots)
 
 
 def moving_rows(dimension):
@@ -403,9 +493,8 @@
     position = base_node.astype(jnp.float32) + offset
     target = jnp.pad(destination[:, 0], (0, spare), constant_values=-1).reshape(chunks, LANES)
     payload = jnp.pad(jnp.concatenate([forces, position], axis=0), ((0, 0), (0, spare)))
-    outgoing, slots = route(target, payload, peer_count, rows)
-    arrived = lax.all_to_all(outgoing, ("gz", "gy"), split_axis=0, concat_axis=0, tiled=True)
-    force_field = spread(arrived, sizes, rows).reshape(3, size_x, size_y, size_z)
+    field, slots, marker_position = outward(target, payload, peer_count, rows, sizes)
+    force_field = field.reshape(3, size_x, size_y, size_z)
     post = collide(populations, force_field)
     moving = moving_rows(0)
     padded = padded_2(jnp.stack([post[index] for index in moving]), (("gx", 1),), 1)
@@ -417,9 +506,7 @@
     padded = padded_2(jnp.stack([post[index] for index in moving]), (("gz", 3),), 1)
     new_populations = shift_along(post, padded, moving, 2, size_z)
     velocity = fluid_velocity(new_populations).reshape(3 * size_x * size_y, size_z)
-    sampled = sample(arrived, velocity, sizes, rows)
-    returned = lax.all_to_all(sampled, ("gz", "gy"), split_axis=0, concat_axis=0, tiled=True)
-    marker_velocity = collect(returned, slots, markers, peer_count, rows)
+    marker_velocity = homeward(marker_position, velocity, slots, markers, rows, sizes)
     return (new_populations, marker_velocity)
 
 

time: 100 us -> 82.6 us (0.83)
  waiting for transfers between devices: 21.6 us -> 3.68 us
  starting transfers between devices: 18.8 us -> 6.48 us
  Pallas kernels: 34.7 us -> 46.7 us
    all_to_all x2 -> x0, waiting for transfers between devices: 17 us -> none  [the longest x1 9.53 us: shards(): lax.all_to_all(outgoing, ('gz', 'gy'), split_axis=0, concat_axis=0, tiled...]
    all_to_all x2 -> x0, starting transfers between devices: 12.3 us -> none  [the longest x1 7.25 us: shards(): lax.all_to_all(outgoing, ('gz', 'gy'), split_axis=0, concat_axis=0, tiled...]
    pallas_call x4 -> x2, Pallas kernels: 34.7 us -> 46.7 us  [the longest x1 28.8 us: outward(): pl.pallas_call(lambda *refs: outward_kernel(peers, rows, sizes, *refs), o...]
    reduce_sum x1, other arithmetic: 0.08 us -> 1.47 us  [collide(): density = jnp.sum(populations, axis=0)]
    ppermute x3, waiting for transfers between devices: 2.48 us -> 1.34 us  [padded_2(): before = lax.ppermute(last, axis, up)]
    ppermute x3, starting transfers between devices: 5.5 us -> 4.39 us  [padded_2(): after = lax.ppermute(initial, axis, down)]
    ppermute x3, starting transfers between devices: 0.98 us -> 2.09 us  [padded_2(): before = lax.ppermute(last, axis, up)]
    unnamed x40 -> x43, local copies, waits for them, and re-layouts: 2.47 us -> 3.06 us
  transfers between devices with their start and end apart: 8 -> 6, of which waited for: 7 -> 5; matrix products, arithmetic and copies ran while one was open for 5% -> 5% of each run, Pallas kernels for 0% -> 0%
where the time goes in v2:
time: 82.6 us; the launch traced here: 82 us
  Pallas kernels  46.7 us (57%)
  local copies, waits for them, and re-layouts  16.1 us (19%)
  other arithmetic  7.92 us (10%)
  starting transfers between devices  6.48 us (8%)
  waiting for transfers between devices  3.68 us (4%)
  between operations  1.1 us (1%)
    pallas_call x1, Pallas kernels, outward(): pl.pallas_call(lambda *refs: outward_kernel(peers, rows, sizes, *refs), o...  28.8 us
    pallas_call x1, Pallas kernels, homeward(): pl.pallas_call(lambda *refs: homeward_kernel(peers, rows, sizes, *refs),...  17.9 us
    ppermute x3, starting transfers between devices, padded_2(): after = lax.ppermute(initial, axis, down)  4.39 us
    slice x3, local copies, waits for them, and re-layouts, padded_2(): last = lax.slice_in_dim(shard, length - width, length, axis=dim)  3.57 us
    unnamed x43, local copies, waits for them, and re-layouts  3.06 us
    unnamed x23, other arithmetic  2.93 us
    ppermute x3, waiting for transfers between devices, padded_2(): after = lax.ppermute(initial, axis, down)  2.34 us
    slice x2, local copies, waits for them, and re-layouts, padded_2(): initial = lax.slice_in_dim(shard, 0, width, axis=dim)  2.24 us
  transfers between devices with their start and end apart: 6, of which 5 were waited for; matrix products, arithmetic and copies ran while one was open for 5% of the time, Pallas kernels for 0%

profile of v2, /device:TPU:0, one launch (start us, length us, event | category | flops | bytes accessed | tf_op | source)
XLA Modules:
  0.0 82.0 jit_solution(5926926149477968970)
XLA Ops:
  0.7 0.8 mul.1658
  1.5 0.8 reduce.19
  2.3 1.0 %reshape.248 = f32[3,8,642]{2,1,0:T(8,128)S(1)} reshape(f32[3,5136]{1,0:T(4,128)} %param.7) | data formatting | bytes 123264 | tf_op jit(solution)/shard_map/reshape | solution.py:53
  3.3 1.5 %reduce_sum.78 = f32[8,16,128]{2,1,0:T(8,128)S(1)} reduce(f32[19,8,16,128]{3,2,1,0:T(8,128)} %param.6, f32[]{:T(128)} %constant.79.clone.1), dimensions={0}, to_apply=%region_0.0 | reduce | flops 294912 | bytes 1310724 | tf_op jit(solution)/shard_map/reduce_sum | solution.py:68
  5.3 28.8 %outward.1 = (f32[384,128]{1,0:T(8,128)S(1)}, s32[2,41,128]{2,1,0:T(8,128)S(1)}, f32[8,33,128]{2,1,0:T(8,128)S(1)}) custom-call(s32[41,128]{1,0:T(8,128)S(1)} %pad_bitcast_fusion.refs_0_, f32[6,5248]{1,0:T(8,128)S(1)} %select_maximum_fusion.refs_1_), custom_call_target="tpu_custom_call" | custom-call | tf_op jit(solution)/shard_map/outward/pallas_call | solution.py:309
  34.1 0.8 %constant_dynamic-update-slice_fusion.29 = (f32[10,8,16,128]{3,2,1,0:T(8,128)S(1)}, f32[1,8,16,128]{3,2,1,0:T(8,128)S(1)}, f32[1,8,16,128]{3,2,1,0:T(8,128)S(1)}...) fusion(f32[1,8,16,128]{3,2,1,0:T(8,128)S(1)} %bitcast.302, ...), kind=kLoop, calls=%fused_computation.44 | loop fusion | flops 1359871 | bytes 1900544
  36.1 0.5 collective-permute-start.1
  36.6 0.8 collective-permute-done
  37.8 0.8 constant_dynamic-update-slice_fusion.10
  38.8 2.0 %collective-permute-start.2 = (f32[10,8,1,128]{3,1,2,0:T(8,128)S(1)}, f32[10,8,1,128]{3,1,2,0:T(8,128)S(1)}, u32[]{:S(2)}, u32[]{:S(2)}) collective-permute-start(f32[10,8,1,128]{3,1,2,0:T(8,128)S(1)} %bitcast.334), channel_id=1, source_target_pairs={{0,2},{2,0},{1,3},{3,1},{4,6},{6,4},{5,7},{7,5},{8,10},{10,8},{9,1... | collective-permute-start | bytes 122888 | tf_op jit(solution)/shard_map/ppermute | solution.py:46
  40.8 2.2 %collective-permute-done.3 = f32[10,8,1,128]{3,1,2,0:T(8,128)S(1)} collective-permute-done((f32[10,8,1,128]{3,1,2,0:T(8,128)S(1)}, f32[10,8,1,128]{3,1,2,0:T(8,128)S(1)}, u32[]{:S(2)}, u32[]{:S(2)}) %collective-permute-start.3) | collective-permute-done | bytes 40992 | tf_op jit(solution)/shard_map/ppermute | solution.py:47
  43.0 0.4 collective-permute-done.2
  43.6 0.7 slice_bitcast_fusion.19
  44.4 1.3 %fusion.149 = (f32[10,8,16,1]{3,2,1,0:T(8,128)}, f32[10,8,16,1]{3,2,1,0:T(8,128)}) fusion(f32[10,8,16,128]{3,2,1,0:T(8,128)S(1)} %constant_dynamic-update-slice_fusion.20), kind=kLoop, calls=%fused_computation.276 | loop fusion | bytes 20480 | tf_op jit(solution)/shard_map/slice | solution.py:44
  45.7 2.2 %copy.116 = f32[10,8,16,1]{2,1,3,0:T(8,128)} copy(f32[10,8,16,1]{3,2,1,0:T(8,128)} %get-tuple-element.48) | data formatting | bytes 10240 | tf_op jit(solution)/shard_map/slice | solution.py:44
  47.9 2.2 %copy.117 = f32[10,8,16,1]{2,1,3,0:T(8,128)} copy(f32[10,8,16,1]{3,2,1,0:T(8,128)} %get-tuple-element.49) | data formatting | bytes 10240 | tf_op jit(solution)/shard_map/slice | solution.py:45
  50.2 3.8 %collective-permute-start.5 = (f32[10,8,16,1]{2,1,3,0:T(8,128)}, f32[10,8,16,1]{2,1,3,0:T(8,128)}, u32[]{:S(2)}, u32[]{:S(2)}) collective-permute-start(f32[10,8,16,1]{2,1,3,0:T(8,128)} %copy.117), channel_id=1, source_target_pairs={{4,0},{8,4},{12,8},{0,12},{5,1},{9,5},{13,9},{1,13},{6,2},{10,6},{... | collective-permute-start | bytes 15368 | tf_op jit(solution)/shard_map/ppermute | solution.py:47
  54.1 2.2 %copy.118 = f32[10,8,16,1]{3,2,1,0:T(8,128)} copy(f32[10,8,16,1]{2,1,3,0:T(8,128)} %collective-permute-done.4) | data formatting | bytes 10240 | tf_op jit(solution)/shard_map/ppermute | solution.py:46
  56.3 2.2 %copy.119 = f32[10,8,16,1]{3,2,1,0:T(8,128)} copy(f32[10,8,16,1]{2,1,3,0:T(8,128)} %collective-permute-done.5) | data formatting | bytes 10240 | tf_op jit(solution)/shard_map/ppermute | solution.py:47
  58.5 1.9 %pad_maximum_fusion = f32[10,8,16,130]{3,2,1,0:T(8,128)S(1)} fusion(f32[10,8,16,1]{3,2,1,0:T(8,128)} %copy.119, f32[10,8,16,128]{3,2,1,0:T(8,128)S(1)} %constant_dynamic-update-slice_fusion.20, f32[10,8,16,1]{3,2,1,0:T(8,128)} %copy.118), kind=kLoop, calls=%fused_computation | loop fusion | flops 332800 | bytes 1331200 | tf_op jit(solution)/shard_map/concatenate | solution.py:48
  60.5 0.7 copy-done.1
  61.8 1.0 %copy-done.9 = f32[19,8,16,128]{3,2,1,0:T(8,128)S(1)} copy-done((f32[19,8,16,128]{3,2,1,0:T(8,128)S(1)}, f32[19,8,16,128]{3,2,1,0:T(8,128)}, u32[]{:S(2)}) %copy-start.9) | copy-done | bytes 1245208
  63.5 17.9 %homeward.1 = f32[3,5136]{1,0:T(4,128)S(1)} custom-call(f32[8,33,128]{2,1,0:T(8,128)S(1)} %get-tuple-element.6.refs_0_, f32[384,128]{1,0:T(8,128)S(1)} %bitcast.285, s32[2,41,128]{2,1,0:T(8,128)S(1)} %get-tuple-element.7.refs_2_), custom_call_target="tpu_custom_call" | custom-call | tf_op jit(solution)/shard_map/homeward/pallas_call | solution.py:446
  81.3 0.6 copy.168
  (86 shorter events, 3.8 us)
Async XLA Ops:
  0.6 4.5 %copy-start.4 = (f32[3,5136]{1,0:T(4,128)S(1)}, f32[3,5136]{1,0:T(4,128)}, u32[]{:S(2)}) copy-start(f32[3,5136]{1,0:T(4,128)} %param.7) | copy-start | bytes 184900
  0.6 4.5 %copy-start.7 = (f32[3,5136]{1,0:T(4,128)S(1)}, f32[3,5136]{1,0:T(4,128)}, u32[]{:S(2)}) copy-start(f32[3,5136]{1,0:T(4,128)} %param.10) | copy-start | bytes 184900
  0.7 4.5 %copy-start.8 = (s32[3,5136]{1,0:T(4,128)S(1)}, s32[3,5136]{1,0:T(4,128)}, u32[]{:S(2)}) copy-start(s32[3,5136]{1,0:T(4,128)} %param.9) | copy-start | bytes 184900
  3.3 30.8 %copy-start = (f32[19,8,16,128]{3,2,1,0:T(8,128)S(1)}, f32[19,8,16,128]{3,2,1,0:T(8,128)}, u32[]{:S(2)}) copy-start(f32[19,8,16,128]{3,2,1,0:T(8,128)} %param.6) | copy-start | bytes 3735556
  36.0 1.3 %collective-permute-start = (f32[10,1,16,128]{3,2,1,0:T(8,128)S(1)}, f32[10,1,16,128]{3,2,1,0:T(8,128)S(1)}, u32[]{:S(2)}, u32[]{:S(2)}) collective-permute-start(f32[10,1,16,128]{3,2,1,0:T(8,128)S(1)} %get-tuple-element.53), channel_id=1, source_target_pairs={{0,1},{1,0},{2,3},{3,2},{4,5},{5,4},{6,7},{7,6},{8,9},{9,8},{10,11... | collective-permute-start | bytes 245768 | tf_op jit(solution)/shard_map/ppermute | solution.py:46
  36.1 1.4 %collective-permute-start.1 = (f32[10,1,16,128]{3,2,1,0:T(8,128)S(1)}, f32[10,1,16,128]{3,2,1,0:T(8,128)S(1)}, u32[]{:S(2)}, u32[]{:S(2)}) collective-permute-start(f32[10,1,16,128]{3,2,1,0:T(8,128)S(1)} %get-tuple-element.52), channel_id=1, source_target_pairs={{1,0},{0,1},{3,2},{2,3},{5,4},{4,5},{7,6},{6,7},{9,8},{8,9},{11,10... | collective-permute-start | bytes 245768 | tf_op jit(solution)/shard_map/ppermute | solution.py:47
  38.7 4.3 %collective-permute-start.3 = (f32[10,8,1,128]{3,1,2,0:T(8,128)S(1)}, f32[10,8,1,128]{3,1,2,0:T(8,128)S(1)}, u32[]{:S(2)}, u32[]{:S(2)}) collective-permute-start(f32[10,8,1,128]{3,1,2,0:T(8,128)S(1)} %bitcast.335), channel_id=1, source_target_pairs={{2,0},{0,2},{3,1},{1,3},{6,4},{4,6},{7,5},{5,7},{10,8},{8,10},{11,... | collective-permute-start | bytes 122888 | tf_op jit(solution)/shard_map/ppermute | solution.py:47
  38.8 4.7 %collective-permute-start.2 = (f32[10,8,1,128]{3,1,2,0:T(8,128)S(1)}, f32[10,8,1,128]{3,1,2,0:T(8,128)S(1)}, u32[]{:S(2)}, u32[]{:S(2)}) collective-permute-start(f32[10,8,1,128]{3,1,2,0:T(8,128)S(1)} %bitcast.334), channel_id=1, source_target_pairs={{0,2},{2,0},{1,3},{3,1},{4,6},{6,4},{5,7},{7,5},{8,10},{10,8},{9,1... | collective-permute-start | bytes 122888 | tf_op jit(solution)/shard_map/ppermute | solution.py:46
  47.9 6.2 %collective-permute-start.4 = (f32[10,8,16,1]{2,1,3,0:T(8,128)}, f32[10,8,16,1]{2,1,3,0:T(8,128)}, u32[]{:S(2)}, u32[]{:S(2)}) collective-permute-start(f32[10,8,16,1]{2,1,3,0:T(8,128)} %copy.116), channel_id=1, source_target_pairs={{0,4},{4,8},{8,12},{12,0},{1,5},{5,9},{9,13},{13,1},{2,6},{6,10},{... | collective-permute-start | bytes 15368 | tf_op jit(solution)/shard_map/ppermute | solution.py:46
  50.2 6.1 %collective-permute-start.5 = (f32[10,8,16,1]{2,1,3,0:T(8,128)}, f32[10,8,16,1]{2,1,3,0:T(8,128)}, u32[]{:S(2)}, u32[]{:S(2)}) collective-permute-start(f32[10,8,16,1]{2,1,3,0:T(8,128)} %copy.117), channel_id=1, source_target_pairs={{4,0},{8,4},{12,8},{0,12},{5,1},{9,5},{13,9},{1,13},{6,2},{10,6},{... | collective-permute-start | bytes 15368 | tf_op jit(solution)/shard_map/ppermute | solution.py:47
  60.3 0.9 %copy-start.1 = (f32[8,18,128]{2,1,0:T(8,128)S(1)}, f32[8,18,128]{2,1,0:T(8,128)}, u32[]{:S(2)}) copy-start(f32[8,18,128]{2,1,0:T(8,128)} %get-tuple-element.42) | copy-start | bytes 221188
  60.3 0.9 %copy-start.2 = (f32[8,18,128]{2,1,0:T(8,128)S(1)}, f32[8,18,128]{2,1,0:T(8,128)}, u32[]{:S(2)}) copy-start(f32[8,18,128]{2,1,0:T(8,128)} %get-tuple-element.47) | copy-start | bytes 221188
  60.3 1.0 %copy-start.3 = (f32[8,18,128]{2,1,0:T(8,128)S(1)}, f32[8,18,128]{2,1,0:T(8,128)}, u32[]{:S(2)}) copy-start(f32[8,18,128]{2,1,0:T(8,128)} %get-tuple-element.38) | copy-start | bytes 221188
  60.3 1.0 %copy-start.5 = (f32[1,8,16,128]{3,2,1,0:T(8,128)S(1)}, f32[1,8,16,128]{3,2,1,0:T(8,128)}, u32[]{:S(2)}) copy-start(f32[1,8,16,128]{3,2,1,0:T(8,128)} %get-tuple-element.18) | copy-start | bytes 196612
  60.4 1.0 %copy-start.6 = (f32[1,8,16,128]{3,2,1,0:T(8,128)S(1)}, f32[1,8,16,128]{3,2,1,0:T(8,128)}, u32[]{:S(2)}) copy-start(f32[1,8,16,128]{3,2,1,0:T(8,128)} %get-tuple-element.20) | copy-start | bytes 196612
  61.5 1.3 %copy-start.9 = (f32[19,8,16,128]{3,2,1,0:T(8,128)S(1)}, f32[19,8,16,128]{3,2,1,0:T(8,128)}, u32[]{:S(2)}) copy-start(f32[19,8,16,128]{3,2,1,0:T(8,128)} %get-tuple-element.22) | copy-start | bytes 3735556
  63.4 18.5 %copy-start.10 = (f32[19,8,16,128]{3,2,1,0:T(8,128)}, f32[19,8,16,128]{3,2,1,0:T(8,128)S(1)}, u32[]{:S(2)}) copy-start(f32[19,8,16,128]{3,2,1,0:T(8,128)S(1)} %constant_dynamic-update-slice_fusion.30) | copy-start | bytes 3735556

commit v3 on v2

--- a/solution.py
+++ b/solution.py
@@ -34,19 +34,7 @@
 WEIGHTS = [1.0 / 3.0] + [1.0 / 18.0] * 6 + [1.0 / 36.0] * 12
 RELAXATION = 0.8
 VELOCITY_UNIT = 0.01
-
-
-def padded_2(shard, sides, width):
-    for axis, dim in sides:
-        size, length = (lax.axis_size(axis), shard.shape[dim])
-        up = [(i, (i + 1) % size) for i in range(size)]
-        down = [(j, i) for i, j in up]
-        last = lax.slice_in_dim(shard, length - width, length, axis=dim)
-        initial = lax.slice_in_dim(shard, 0, width, axis=dim)
-        before = lax.ppermute(last, axis, up)
-        after = lax.ppermute(initial, axis, down)
-        shard = jnp.concatenate([before, shard, after], axis=dim)
-    return shard
+MESH = pl.DeviceIdType.MESH
 
 
 def marker_forces(displacement, stiffness):
@@ -65,7 +53,7 @@
 
 
 def collide(populations, force_field):
-    density = jnp.sum(populations, axis=0)
+    density = sum(populations[1:], populations[0])
     velocity = [
         (momentum_sum(populations, dimension) + 0.5 * force_field[dimension]) / density
         for dimension in range(3)
@@ -101,12 +89,157 @@
             - (populations[index] - equilibrium) / RELAXATION
             + factor * WEIGHTS[index] * source
         )
-    return jnp.stack(result)
-
-
-def fluid_velocity(populations):
-    density = jnp.sum(populations, axis=0)
-    return jnp.stack([momentum_sum(populations, dimension) / density for dimension in range(3)])
+    return result
+
+
+def directions(dimension, sign):
+    return [index for index in range(19) if int(LATTICE[index][dimension]) == sign]
+
+
+AXES = ("gx", "gy", "gz")
+FACES = [(dimension, sign) for dimension in range(3) for sign in (1, -1)]
+
+
+def neighbour(dimension, sign):
+    size = lax.axis_size(AXES[dimension])
+    return {AXES[dimension]: lax.rem(lax.axis_index(AXES[dimension]) + size + sign, size)}
+
+
+def fluid_kernel(
+    populations_ref, field_ref, result_ref, velocity_ref,
+    out_x, out_y, out_z, in_x, in_y, in_z, send_sem, recv_sem,
+):
+    size_x, size_y, size_z = populations_ref.shape[1:]
+    barrier = pltpu.get_barrier_semaphore()
+    for face in FACES:
+        pl.semaphore_signal(barrier, inc=1, device_id=neighbour(*face), device_id_type=MESH)
+
+    def collided(x):
+        return collide(
+            [populations_ref[index, x] for index in range(19)],
+            [field_ref[dimension, x] for dimension in range(3)],
+        )
+
+    def copy(face, source, target):
+        dimension, sign = FACES[face]
+        return pltpu.make_async_remote_copy(
+            src_ref=source.at[face % 2],
+            dst_ref=target.at[face % 2],
+            send_sem=send_sem.at[face],
+            recv_sem=recv_sem.at[face],
+            device_id=neighbour(dimension, sign),
+            device_id_type=MESH,
+        )
+
+    first, last = collided(0), collided(size_x - 1)
+    for slot, index in enumerate(directions(0, 1)):
+        out_x[0, slot] = last[index]
+        result_ref[index, 1] = first[index]
+    for slot, index in enumerate(directions(0, -1)):
+        out_x[1, slot] = first[index]
+        result_ref[index, size_x - 2] = last[index]
+    for index in directions(0, 0):
+        result_ref[index, 0] = first[index]
+        result_ref[index, size_x - 1] = last[index]
+    pl.semaphore_wait(barrier, len(FACES))
+    copies = [copy(face, out_x, in_x) for face in (0, 1)]
+    for one in copies:
+        one.start()
+
+    def inner(x, carry):
+        post = collided(x)
+        for index in range(19):
+            result_ref[index, x + int(LATTICE[index][0])] = post[index]
+        return carry
+
+    lax.fori_loop(1, size_x - 1, inner, 0)
+    for one in copies:
+        one.wait_recv()
+    for slot, index in enumerate(directions(0, 1)):
+        result_ref[index, 0] = in_x[0, slot]
+    for slot, index in enumerate(directions(0, -1)):
+        result_ref[index, size_x - 1] = in_x[1, slot]
+
+    for side, sign in enumerate((1, -1)):
+        edge = size_y - 1 if sign == 1 else 0
+        for slot, index in enumerate(directions(1, sign)):
+            out_y[side, slot] = jnp.concatenate(
+                [result_ref[index, x, edge : edge + 1, :] for x in range(size_x)], axis=0
+            )
+    copies_y = [copy(face, out_y, in_y) for face in (2, 3)]
+    for one in copies_y:
+        one.start()
+    for one in copies_y:
+        one.wait_recv()
+    for side, sign in enumerate((1, -1)):
+        for slot, index in enumerate(directions(1, sign)):
+            for x in range(size_x):
+                plane = result_ref[index, x]
+                row = in_y[side, slot, x : x + 1, :]
+                result_ref[index, x] = jnp.concatenate(
+                    [row, plane[: size_y - 1]] if sign == 1 else [plane[1:], row], axis=0
+                )
+
+    lane = iota((size_y, size_z), 1)
+    for side, sign in enumerate((1, -1)):
+        edge = size_z - 1 if sign == 1 else 0
+        packed = jnp.zeros((size_y, size_z), jnp.float32)
+        for slot, index in enumerate(directions(2, sign)):
+            for x in range(size_x):
+                packed = jnp.where(
+                    lane == slot * size_x + x, result_ref[index, x, :, edge : edge + 1], packed
+                )
+        out_z[side] = packed
+    copies_z = [copy(face, out_z, in_z) for face in (4, 5)]
+    for one in copies_z:
+        one.start()
+    for one in copies_z:
+        one.wait_recv()
+    for side, sign in enumerate((1, -1)):
+        edge = 0 if sign == 1 else size_z - 1
+        arrived = in_z[side]
+        for slot, index in enumerate(directions(2, sign)):
+            for x in range(size_x):
+                at = slot * size_x + x
+                turned = pltpu.roll(result_ref[index, x], 1 if sign == 1 else size_z - 1, axis=1)
+                result_ref[index, x] = jnp.where(lane == edge, arrived[:, at : at + 1], turned)
+
+    def speed(x, carry):
+        planes = [result_ref[index, x] for index in range(19)]
+        density = sum(planes[1:], planes[0])
+        for dimension in range(3):
+            velocity_ref[dimension, x] = momentum_sum(planes, dimension) / density
+        return carry
+
+    lax.fori_loop(0, size_x, speed, 0)
+    for one in copies + copies_y + copies_z:
+        one.wait_send()
+
+
+def fluid(populations, force_field):
+    size_x, size_y, size_z = populations.shape[1:]
+    moving = len(directions(0, 1))
+    assert moving * size_x <= size_z
+    faces = [
+        (2, moving, size_y, size_z),
+        (2, moving, size_x, size_z),
+        (2, size_y, size_z),
+    ]
+    return pl.pallas_call(
+        fluid_kernel,
+        out_shape=(
+            jax.ShapeDtypeStruct(populations.shape, jnp.float32),
+            jax.ShapeDtypeStruct((3, size_x, size_y, size_z), jnp.float32),
+        ),
+        in_specs=[pl.BlockSpec(memory_space=pltpu.VMEM)] * 2,
+        out_specs=(pl.BlockSpec(memory_space=pltpu.VMEM),) * 2,
+        scratch_shapes=[pltpu.VMEM(shape, jnp.float32) for shape in faces + faces]
+        + [pltpu.SemaphoreType.DMA((len(FACES),)), pltpu.SemaphoreType.DMA((len(FACES),))],
+        compiler_params=pltpu.CompilerParams(
+            vmem_limit_bytes=VMEM_LIMIT, collective_id=2, has_side_effects=True
+        ),
+        name="fluid",
+    )(populations, force_field)
 
 
 LANES = 128
@@ -124,7 +257,6 @@
     return high, (value - high.astype(jnp.float32)).astype(jnp.bfloat16)
 
 
-MESH = pl.DeviceIdType.MESH
 PEERS = ("gz", "gy")
 
 
@@ -466,20 +598,6 @@
     )(position, velocity, slots)
 
 
-def moving_rows(dimension):
-    return [index for index in range(19) if int(LATTICE[index][dimension]) != 0]
-
-
-def shift_along(field, padded, moving, dimension, length):
-    pieces = [field[index] for index in range(19)]
-    for slot_pos, index in enumerate(moving):
-        first_cell = 1 - int(LATTICE[index][dimension])
-        pieces[index] = lax.slice_in_dim(
-            padded[slot_pos], first_cell, first_cell + length, axis=dimension
-        )
-    return jnp.stack(pieces)
-
-
 def shards(populations, displacement, stiffness, base_node, offset, destination):
     size_x, size_y, size_z = (populations.shape[1], populations.shape[2], populations.shape[3])
     peer_count = lax.axis_size(("gz", "gy"))
@@ -495,17 +613,8 @@
     payload = jnp.pad(jnp.concatenate([forces, position], axis=0), ((0, 0), (0, spare)))
     field, slots, marker_position = outward(target, payload, peer_count, rows, sizes)
     force_field = field.reshape(3, size_x, size_y, size_z)
-    post = collide(populations, force_field)
-    moving = moving_rows(0)
-    padded = padded_2(jnp.stack([post[index] for index in moving]), (("gx", 1),), 1)
-    post = shift_along(post, padded, moving, 0, size_x)
-    moving = moving_rows(1)
-    padded = padded_2(jnp.stack([post[index] for index in moving]), (("gy", 2),), 1)
-    post = shift_along(post, padded, moving, 1, size_y)
-    moving = moving_rows(2)
-    padded = padded_2(jnp.stack([post[index] for index in moving]), (("gz", 3),), 1)
-    new_populations = shift_along(post, padded, moving, 2, size_z)
-    velocity = fluid_velocity(new_populations).reshape(3 * size_x * size_y, size_z)
+    new_populations, velocity = fluid(populations, force_field)
+    velocity = velocity.reshape(3 * size_x * size_y, size_z)
     marker_velocity = homeward(marker_position, velocity, slots, markers, rows, sizes)
     return (new_populations, marker_velocity)
 

time: 82.6 us -> 60.7 us (0.73)
  local copies, waits for them, and re-layouts: 16.1 us -> 3.81 us
  Pallas kernels: 46.7 us -> 54.7 us
  other arithmetic: 7.92 us -> 1.22 us
  starting transfers between devices: 6.48 us -> 0 us
  waiting for transfers between devices: 3.68 us -> 0 us
    pallas_call x0 -> x1, Pallas kernels: none -> 9.45 us  [fluid(): pl.pallas_call(fluid_kernel, out_shape=(jax.ShapeDtypeStruct(populations....]
    ppermute x6 -> x0, starting transfers between devices: 6.48 us -> none  [the longest x3 4.39 us: padded_2(): after = lax.ppermute(initial, axis, down)]
    slice x6 -> x0, local copies, waits for them, and re-layouts: 5.82 us -> none  [the longest x3 3.57 us: padded_2(): last = lax.slice_in_dim(shard, length - width, length, axis=dim)]
    ppermute x2 -> x0, local copies, waits for them, and re-layouts: 4.33 us -> none  [the longest x1 2.17 us: padded_2(): before = lax.ppermute(last, axis, up)]
    ppermute x6 -> x0, waiting for transfers between devices: 3.68 us -> none  [the longest x3 2.34 us: padded_2(): after = lax.ppermute(initial, axis, down)]
    unnamed x23 -> x1, other arithmetic: 2.93 us -> 0.05 us
    concatenate x2 -> x0, other arithmetic: 2.02 us -> none  [padded_2(): shard = jnp.concatenate([before, shard, after], axis=dim)]
    reduce_sum x1 -> x0, other arithmetic: 1.47 us -> none  [collide(): density = jnp.sum(populations, axis=0)]
  transfers between devices with their start and end apart: 6 -> 0, of which waited for: 5 -> 0; matrix products, arithmetic and copies ran while one was open for 5% -> 0% of each run, Pallas kernels for 0% -> 0%
where the time goes in v3:
time: 60.7 us; the launch traced here: 60.5 us
  Pallas kernels  54.7 us (90%)
  local copies, waits for them, and re-layouts  3.81 us (6%)
  other arithmetic  1.22 us (2%)
  between operations  0.73 us (1%)
    pallas_call x1, Pallas kernels, outward(): pl.pallas_call(lambda *refs: outward_kernel(peers, rows, sizes, *refs), o...  28.8 us
    pallas_call x1, Pallas kernels, homeward(): pl.pallas_call(lambda *refs: homeward_kernel(peers, rows, sizes, *refs),...  16.5 us
    pallas_call x1, Pallas kernels, fluid(): pl.pallas_call(fluid_kernel, out_shape=(jax.ShapeDtypeStruct(populations....  9.45 us
    unnamed x6, local copies, waits for them, and re-layouts  1.68 us

profile of v3, /device:TPU:0, one launch (start us, length us, event | category | flops | bytes accessed | tf_op | source)
XLA Modules:
  0.0 60.5 jit_solution(12649820678392590416)
XLA Ops:
  0.6 0.0 copy-start.1
  0.6 0.0 copy-start
  0.6 1.1 %reshape.25 = f32[3,8,642]{2,1,0:T(8,128)S(1)} reshape(f32[3,5136]{1,0:T(4,128)} %param.7) | data formatting | bytes 123264 | tf_op jit(solution)/shard_map/reshape | solution.py:41
  1.8 0.1 reduce_sum.9
  1.9 0.1 sub.11
  1.9 0.1 sub.12
  2.1 0.7 %mul.13 = f32[8,642]{1,0:T(8,128)S(1)} broadcast(f32[8]{0:T(128)} %param.8), dimensions={0} | broadcast | bytes 20576 | tf_op jit(solution)/shard_map/mul | solution.py:43
  2.8 0.1 mul.14
  2.9 1.0 %convert_add_fusion = (f32[3,5136]{1,0:T(4,128)S(1)}, f32[3,5136]{1,0:T(4,128)S(1)}) fusion(f32[3,5136]{1,0:T(4,128)} %param.10, s32[3,5136]{1,0:T(4,128)} %param.9, f32[3,5136]{1,0:T(4,128)} %param.7, f32[3,5136]{1,0:T(4,128)S(1)} %sub.12, f32[5136]{0:T(1024)S(1)} %mul.14), kind=kLoop, calls=%fused_computation.2 | loop fusion | flops 61632 | bytes 390336 | tf_op jit(solution)/shard_map/add | solution.py:611
  4.0 0.0 copy-done.1
  4.0 0.1 reduce
  4.1 28.8 %outward.1 = (f32[384,128]{1,0:T(8,128)S(1)}, s32[2,41,128]{2,1,0:T(8,128)S(1)}, f32[8,33,128]{2,1,0:T(8,128)S(1)}) custom-call(s32[41,128]{1,0:T(8,128)S(1)} %pad_bitcast_fusion.refs_0_, f32[6,5248]{1,0:T(8,128)S(1)} %select_maximum_fusion.refs_1_), custom_call_target="tpu_custom_call" | custom-call | tf_op jit(solution)/shard_map/outward/pallas_call | solution.py:441
  32.9 0.0 copy-done
  32.9 9.5 %fluid.1 = (f32[19,8,16,128]{3,2,1,0:T(8,128)S(1)}, f32[3,8,16,128]{3,2,1,0:T(8,128)S(1)}) custom-call(f32[19,8,16,128]{3,2,1,0:T(8,128)S(1)} %copy-done, f32[3,8,16,128]{3,2,1,0:T(8,128)S(1)} %bitcast.5), custom_call_target="tpu_custom_call" | custom-call | tf_op jit(solution)/shard_map/fluid/pallas_call | solution.py:228
  42.3 16.5 %homeward.1 = f32[3,5136]{1,0:T(4,128)S(1)} custom-call(f32[8,33,128]{2,1,0:T(8,128)S(1)} %get-tuple-element.9.refs_0_, f32[384,128]{1,0:T(8,128)S(1)} %bitcast.4, s32[2,41,128]{2,1,0:T(8,128)S(1)} %get-tuple-element.11.refs_2_), custom_call_target="tpu_custom_call" | custom-call | tf_op jit(solution)/shard_map/homeward/pallas_call | solution.py:578
  58.8 1.0 %copy.10 = f32[19,8,16,128]{3,2,1,0:T(8,128)} copy(f32[19,8,16,128]{3,2,1,0:T(8,128)S(1)} %get-tuple-element.16) | data formatting | bytes 2490368
  59.8 0.6 %copy.11 = f32[3,5136]{1,0:T(4,128)} copy(f32[3,5136]{1,0:T(4,128)S(1)} %homeward.1) | data formatting | bytes 123264
  (3 shorter events, 0.1 us)
Async XLA Ops:
  0.6 3.3 %copy-start.1 = (s32[5136,1]{0,1:T(1,128)S(1)}, s32[5136,1]{0,1:T(1,128)}, u32[]{:S(2)}) copy-start(s32[5136,1]{0,1:T(1,128)} %param.11) | copy-start | bytes 61636
  0.6 32.2 %copy-start = (f32[19,8,16,128]{3,2,1,0:T(8,128)S(1)}, f32[19,8,16,128]{3,2,1,0:T(8,128)}, u32[]{:S(2)}) copy-start(f32[19,8,16,128]{3,2,1,0:T(8,128)} %populations_ref.1) | copy-start | bytes 3735556

commit v4 on v3

--- a/solution.py
+++ b/solution.py
@@ -313,14 +313,20 @@
         return jnp.where(mask, within + before, rank)
 
     rank = lax.fori_loop(0, peers, ranked, jnp.zeros(target.shape, jnp.float32)).astype(jnp.int32)
-    slot_ref[0] = jnp.where(target < 0, -1, target * rows + lax.div(rank, LANES))
-    slot_ref[1] = lax.rem(rank, LANES)
+    halves = (rows + 1) // 2
+    wide = lax.div(rank, 2 * LANES)
+    within = rank - 2 * LANES * wide
+    right_half = (within >= LANES).astype(jnp.int32)
+    slot_ref[0] = jnp.where(target < 0, -1, target * rows + right_half * halves + wide)
+    slot_ref[1] = within - LANES * right_half
+    slot_ref[2] = jnp.where(target < 0, -1, target * halves + wide)
+    slot_ref[3] = within
     height = left_ref.shape[0] // 15
 
     def place(chunk, carry):
         at = pl.ds(pl.multiple_of(chunk * LANES, LANES), LANES)
-        high_mask = iota((height, LANES), 0) == slot_ref[0, pl.ds(chunk, 1), :]
-        low_mask = iota((LANES, LANES), 0) == slot_ref[1, pl.ds(chunk, 1), :]
+        high_mask = iota((height, LANES), 0) == slot_ref[2, pl.ds(chunk, 1), :]
+        low_mask = iota((2 * LANES, LANES), 0) == slot_ref[3, pl.ds(chunk, 1), :]
         right_ref[:, at] = low_mask.astype(jnp.float32).astype(bf16)
         values = payload_ref[:, at]
         first = values.astype(bf16).astype(jnp.float32)
@@ -348,7 +354,12 @@
             total = total + placed[(piece + more) * height : (piece + more + 1) * height]
         piece += count
         for peer in range(peers):
-            sent_ref[peer, row * rows : (row + 1) * rows, :] = total[peer * rows : (peer + 1) * rows]
+            first, middle = peer * halves, row * rows + halves
+            sent_ref[peer, row * rows : middle, :] = total[first : first + halves, :LANES]
+            if rows > halves:
+                sent_ref[peer, middle : (row + 1) * rows, :] = total[
+                    first : first + rows - halves, LANES:
+                ]
 
 
 def stencil(position):
@@ -367,7 +378,7 @@
     return result
 
 
-def spread_part(sizes, rows, block, left_ref, right_ref, total_ref):
+def spread_build(sizes, rows, block, left_ref, right_ref):
     size_x, size_y, size_z = sizes
     height = 3 * size_x * size_y
     base, weights = stencil(block[3 * rows : 6 * rows])
@@ -385,6 +396,9 @@
                 high, low = split_two(along_y * scaled[x : x + 1, :])
                 left_ref[first : first + size_y, at] = high
                 left_ref[height + first : height + first + size_y, at] = low
+
+
+def spread_add(left_ref, right_ref, total_ref):
     total_ref[...] += lax.dot_general(
         left_ref[...], right_ref[...], NT, preferred_element_type=jnp.float32
     )
@@ -392,7 +406,7 @@
 
 def outward_kernel(
     peers, rows, sizes, target_ref, payload_ref, field_ref, slot_ref, position_ref,
-    route_left, route_right, sent_ref, arrived_ref, left_ref, right_ref, total_ref,
+    route_left, route_right, sent_ref, arrived_ref, left_ref, right_ref, left_other, right_other, total_ref,
     send_sem, recv_sem,
 ):
     me = lax.axis_index(PEERS)
@@ -410,19 +424,28 @@
     lax.fori_loop(1, peers, send, 0)
     total_ref[...] = jnp.zeros_like(total_ref)
 
-    def add(source, block):
+    buffers = [(left_ref, right_ref), (left_other, right_other)]
+
+    def build(source, block, buffer):
         position_ref[source] = block[3 * rows : 6 * rows]
-        spread_part(sizes, rows, block, left_ref, right_ref, total_ref)
-
-    add(me, sent_ref[me])
-
-    def one(step, carry):
+        spread_build(sizes, rows, block, *buffer)
+
+    def one(step, built):
         copy(step).wait_recv()
         source = lax.rem(me + peers - step, peers)
-        add(source, arrived_ref[source])
-        return carry
-
-    lax.fori_loop(1, peers, one, 0)
+        spread_add(*buffers[built], total_ref)
+        build(source, arrived_ref[source], buffers[1 - built])
+
+    def two(pair, carry):
+        one(2 * pair + 1, 0)
+        one(2 * pair + 2, 1)
+        return carry
+
+    build(me, sent_ref[me], buffers[0])
+    lax.fori_loop(0, (peers - 1) // 2, two, 0)
+    if peers % 2 == 0:
+        one(peers - 1, 0)
+    spread_add(*buffers[1 - peers % 2], total_ref)
     field_ref[...] = (total_ref[height:, size_z:] + total_ref[height:, :size_z]) + (
         total_ref[:height, size_z:] + total_ref[:height, :size_z]
     )
@@ -436,22 +459,24 @@
 
 def outward(target, payload, peers, rows, sizes):
     chunks = target.shape[0]
-    slots_high = -(-peers * rows // 16) * 16
+    slots_high = -(-peers * ((rows + 1) // 2) // 16) * 16
     height = 3 * sizes[0] * sizes[1]
     return pl.pallas_call(
         lambda *refs: outward_kernel(peers, rows, sizes, *refs),
         out_shape=(
             jax.ShapeDtypeStruct((height, sizes[2]), jnp.float32),
-            jax.ShapeDtypeStruct((2, chunks, LANES), jnp.int32),
+            jax.ShapeDtypeStruct((4, chunks, LANES), jnp.int32),
             jax.ShapeDtypeStruct((peers, 3 * rows, LANES), jnp.float32),
         ),
         in_specs=[pl.BlockSpec(memory_space=pltpu.VMEM)] * 2,
         out_specs=(pl.BlockSpec(memory_space=pltpu.VMEM),) * 3,
         scratch_shapes=[
             pltpu.VMEM((15 * slots_high, chunks * LANES), jnp.bfloat16),
-            pltpu.VMEM((LANES, chunks * LANES), jnp.bfloat16),
+            pltpu.VMEM((2 * LANES, chunks * LANES), jnp.bfloat16),
             pltpu.VMEM((peers, 6 * rows, LANES), jnp.float32),
             pltpu.VMEM((peers, 6 * rows, LANES), jnp.float32),
+            pltpu.VMEM((2 * height, rows * LANES), jnp.bfloat16),
+            pltpu.VMEM((2 * sizes[2], rows * LANES), jnp.bfloat16),
             pltpu.VMEM((2 * height, rows * LANES), jnp.bfloat16),
             pltpu.VMEM((2 * sizes[2], rows * LANES), jnp.bfloat16),
             pltpu.VMEM((2 * height, 2 * sizes[2]), jnp.float32),
@@ -503,8 +528,13 @@
     left_ref[:, :LANES] = high
     left_ref[:, LANES:] = low
 
-    def one(chunk):
-        low_mask = iota((LANES, LANES), 0) == slot_ref[1, pl.ds(chunk, 1), :]
+    def one(chunk, count):
+        width = count * LANES
+        wide = [
+            jnp.concatenate([slot_ref[part, pl.ds(chunk + j, 1), :] for j in range(count)], axis=1)
+            for part in range(2)
+        ]
+        low_mask = iota((LANES, width), 0) == wide[1]
         onehot = low_mask.astype(jnp.float32).astype(jnp.bfloat16)
         found = lax.dot_general(
             left_ref[...],
@@ -512,7 +542,7 @@
             NN,
             preferred_element_type=jnp.float32,
         )
-        high_mask = iota((height, LANES), 0) == slot_ref[0, pl.ds(chunk, 1), :]
+        high_mask = iota((height, width), 0) == wide[0]
         return jnp.concatenate(
             [
                 jnp.sum(
@@ -527,13 +557,16 @@
 
     whole, rest = markers // LANES, markers % LANES
 
-    def step(chunk, carry):
-        result_ref[:, pl.ds(pl.multiple_of(chunk * LANES, LANES), LANES)] = one(chunk)
-        return carry
-
-    lax.fori_loop(0, whole, step, 0, unroll=4)
+    def step(pair, carry):
+        at = pl.ds(pl.multiple_of(2 * pair * LANES, 2 * LANES), 2 * LANES)
+        result_ref[:, at] = one(2 * pair, 2)
+        return carry
+
+    lax.fori_loop(0, whole // 2, step, 0, unroll=2)
+    if whole % 2:
+        result_ref[:, (whole - 1) * LANES : whole * LANES] = one(whole - 1, 1)
     if rest:
-        result_ref[:, markers - rest :] = one(whole)[:, :rest]
+        result_ref[:, markers - rest :] = one(whole, 1)[:, :rest]
 
 
 def homeward_kernel(

time: 60.7 us -> 55.3 us (0.911)
  Pallas kernels: 54.7 us -> 49.4 us
    pallas_call x1, Pallas kernels: 28.8 us -> 24.1 us  [outward(): pl.pallas_call(lambda *refs: outward_kernel(peers, rows, sizes, *refs), o...]
    pallas_call x1, Pallas kernels: 16.5 us -> 15.6 us  [homeward(): pl.pallas_call(lambda *refs: homeward_kernel(peers, rows, sizes, *refs),...]
where the time goes in v4:
time: 55.3 us; the launch traced here: 55.1 us
  Pallas kernels  49.4 us (89%)
  local copies, waits for them, and re-layouts  3.81 us (7%)
  other arithmetic  1.22 us (2%)
  between operations  0.73 us (1%)
    pallas_call x1, Pallas kernels, outward(): pl.pallas_call(lambda *refs: outward_kernel(peers, rows, sizes, *refs), o...  24.1 us
    pallas_call x1, Pallas kernels, homeward(): pl.pallas_call(lambda *refs: homeward_kernel(peers, rows, sizes, *refs),...  15.6 us
    pallas_call x1, Pallas kernels, fluid(): pl.pallas_call(fluid_kernel, out_shape=(jax.ShapeDtypeStruct(populations....  9.69 us
    unnamed x6, local copies, waits for them, and re-layouts  1.68 us

profile of v4, /device:TPU:0, one launch (start us, length us, event | category | flops | bytes accessed | tf_op | source)
XLA Modules:
  0.0 55.1 jit_solution(10049570197505046567)
XLA Ops:
  0.6 0.0 copy-start.1
  0.6 0.0 copy-start
  0.6 1.1 %reshape.25 = f32[3,8,642]{2,1,0:T(8,128)S(1)} reshape(f32[3,5136]{1,0:T(4,128)} %param.7) | data formatting | bytes 123264 | tf_op jit(solution)/shard_map/reshape | solution.py:41
  1.8 0.1 reduce_sum.9
  1.9 0.1 sub.11
  1.9 0.1 sub.12
  2.1 0.7 %mul.13 = f32[8,642]{1,0:T(8,128)S(1)} broadcast(f32[8]{0:T(128)} %param.8), dimensions={0} | broadcast | bytes 20576 | tf_op jit(solution)/shard_map/mul | solution.py:43
  2.8 0.1 mul.14
  2.9 1.0 %convert_add_fusion = (f32[3,5136]{1,0:T(4,128)S(1)}, f32[3,5136]{1,0:T(4,128)S(1)}) fusion(f32[3,5136]{1,0:T(4,128)} %param.10, s32[3,5136]{1,0:T(4,128)} %param.9, f32[3,5136]{1,0:T(4,128)} %param.7, f32[3,5136]{1,0:T(4,128)S(1)} %sub.12, f32[5136]{0:T(1024)S(1)} %mul.14), kind=kLoop, calls=%fused_computation.2 | loop fusion | flops 61632 | bytes 390336 | tf_op jit(solution)/shard_map/add | solution.py:644
  4.0 0.0 copy-done.1
  4.0 0.1 reduce
  4.1 24.1 %outward.1 = (f32[384,128]{1,0:T(8,128)S(1)}, s32[4,41,128]{2,1,0:T(8,128)S(1)}, f32[8,33,128]{2,1,0:T(8,128)S(1)}) custom-call(s32[41,128]{1,0:T(8,128)S(1)} %pad_bitcast_fusion.refs_0_, f32[6,5248]{1,0:T(8,128)S(1)} %select_maximum_fusion.refs_1_), custom_call_target="tpu_custom_call" | custom-call | tf_op jit(solution)/shard_map/outward/pallas_call | solution.py:464
  28.2 0.0 copy-done
  28.2 9.7 %fluid.1 = (f32[19,8,16,128]{3,2,1,0:T(8,128)S(1)}, f32[3,8,16,128]{3,2,1,0:T(8,128)S(1)}) custom-call(f32[19,8,16,128]{3,2,1,0:T(8,128)S(1)} %copy-done, f32[3,8,16,128]{3,2,1,0:T(8,128)S(1)} %bitcast.5), custom_call_target="tpu_custom_call" | custom-call | tf_op jit(solution)/shard_map/fluid/pallas_call | solution.py:228
  37.9 15.6 %homeward.1 = f32[3,5136]{1,0:T(4,128)S(1)} custom-call(f32[8,33,128]{2,1,0:T(8,128)S(1)} %get-tuple-element.9.refs_0_, f32[384,128]{1,0:T(8,128)S(1)} %bitcast.4, s32[4,41,128]{2,1,0:T(8,128)S(1)} %get-tuple-element.11.refs_2_), custom_call_target="tpu_custom_call" | custom-call | tf_op jit(solution)/shard_map/homeward/pallas_call | solution.py:611
  53.5 1.0 %copy.10 = f32[19,8,16,128]{3,2,1,0:T(8,128)} copy(f32[19,8,16,128]{3,2,1,0:T(8,128)S(1)} %get-tuple-element.16) | data formatting | bytes 2490368
  54.5 0.6 %copy.11 = f32[3,5136]{1,0:T(4,128)} copy(f32[3,5136]{1,0:T(4,128)S(1)} %homeward.1) | data formatting | bytes 123264
  (3 shorter events, 0.1 us)
Async XLA Ops:
  0.6 3.3 %copy-start.1 = (s32[5136,1]{0,1:T(1,128)S(1)}, s32[5136,1]{0,1:T(1,128)}, u32[]{:S(2)}) copy-start(s32[5136,1]{0,1:T(1,128)} %param.11) | copy-start | bytes 61636
  0.6 27.6 %copy-start = (f32[19,8,16,128]{3,2,1,0:T(8,128)S(1)}, f32[19,8,16,128]{3,2,1,0:T(8,128)}, u32[]{:S(2)}) copy-start(f32[19,8,16,128]{3,2,1,0:T(8,128)} %populations_ref.1) | copy-start | bytes 3735556

commit v5 on v4

--- a/solution.py
+++ b/solution.py
@@ -211,7 +211,7 @@
             velocity_ref[dimension, x] = momentum_sum(planes, dimension) / density
         return carry
 
-    lax.fori_loop(0, size_x, speed, 0)
+    lax.fori_loop(0, size_x, speed, 0, unroll=2)
     for one in copies + copies_y + copies_z:
         one.wait_send()
 
@@ -342,7 +342,7 @@
                 piece += 1
         return carry
 
-    lax.fori_loop(0, chunks, place, 0)
+    lax.fori_loop(0, chunks, place, 0, unroll=4)
     placed = lax.dot_general(
         left_ref[...], right_ref[...], NT, preferred_element_type=jnp.float32
     )
@@ -562,7 +562,7 @@
         result_ref[:, at] = one(2 * pair, 2)
         return carry
 
-    lax.fori_loop(0, whole // 2, step, 0, unroll=2)
+    lax.fori_loop(0, whole // 2, step, 0, unroll=4)
     if whole % 2:
         result_ref[:, (whole - 1) * LANES : whole * LANES] = one(whole - 1, 1)
     if rest:

time: 55.3 us -> 54.9 us (level)
    pallas_call x1, Pallas kernels: 15.6 us -> 14.7 us  [homeward(): pl.pallas_call(lambda *refs: homeward_kernel(peers, rows, sizes, *refs),...]
where the time goes in v5:
time: 54.9 us; the launch traced here: 54.7 us
  Pallas kernels  48.9 us (89%)
  local copies, waits for them, and re-layouts  3.81 us (7%)
  other arithmetic  1.22 us (2%)
  between operations  0.73 us (1%)
    pallas_call x1, Pallas kernels, outward(): pl.pallas_call(lambda *refs: outward_kernel(peers, rows, sizes, *refs), o...  24.5 us
    pallas_call x1, Pallas kernels, homeward(): pl.pallas_call(lambda *refs: homeward_kernel(peers, rows, sizes, *refs),...  14.7 us
    pallas_call x1, Pallas kernels, fluid(): pl.pallas_call(fluid_kernel, out_shape=(jax.ShapeDtypeStruct(populations....  9.63 us
    unnamed x6, local copies, waits for them, and re-layouts  1.68 us
    reshape x1, local copies, waits for them, and re-layouts, marker_forces(): grouped = displacement.reshape(3, stiffness.shape[0], -1)  1.1 us

profile of v5, /device:TPU:0, one launch (start us, length us, event | category | flops | bytes accessed | tf_op | source)
XLA Modules:
  0.0 54.7 jit_solution(86242915553160450)
XLA Ops:
  0.6 0.0 copy-start.1
  0.6 0.0 copy-start
  0.6 1.1 %reshape.25 = f32[3,8,642]{2,1,0:T(8,128)S(1)} reshape(f32[3,5136]{1,0:T(4,128)} %param.7) | data formatting | bytes 123264 | tf_op jit(solution)/shard_map/reshape | solution.py:41
  1.8 0.1 reduce_sum.9
  1.9 0.1 sub.11
  1.9 0.1 sub.12
  2.1 0.7 %mul.13 = f32[8,642]{1,0:T(8,128)S(1)} broadcast(f32[8]{0:T(128)} %param.8), dimensions={0} | broadcast | bytes 20576 | tf_op jit(solution)/shard_map/mul | solution.py:43
  2.8 0.1 mul.14
  2.9 1.0 %convert_add_fusion = (f32[3,5136]{1,0:T(4,128)S(1)}, f32[3,5136]{1,0:T(4,128)S(1)}) fusion(f32[3,5136]{1,0:T(4,128)} %param.10, s32[3,5136]{1,0:T(4,128)} %param.9, f32[3,5136]{1,0:T(4,128)} %param.7, f32[3,5136]{1,0:T(4,128)S(1)} %sub.12, f32[5136]{0:T(1024)S(1)} %mul.14), kind=kLoop, calls=%fused_computation.2 | loop fusion | flops 61632 | bytes 390336 | tf_op jit(solution)/shard_map/add | solution.py:644
  4.0 0.0 copy-done.1
  4.0 0.1 reduce
  4.1 24.5 %outward.1 = (f32[384,128]{1,0:T(8,128)S(1)}, s32[4,41,128]{2,1,0:T(8,128)S(1)}, f32[8,33,128]{2,1,0:T(8,128)S(1)}) custom-call(s32[41,128]{1,0:T(8,128)S(1)} %pad_bitcast_fusion.refs_0_, f32[6,5248]{1,0:T(8,128)S(1)} %select_maximum_fusion.refs_1_), custom_call_target="tpu_custom_call" | custom-call | tf_op jit(solution)/shard_map/outward/pallas_call | solution.py:464
  28.6 0.0 copy-done
  28.6 9.6 %fluid.1 = (f32[19,8,16,128]{3,2,1,0:T(8,128)S(1)}, f32[3,8,16,128]{3,2,1,0:T(8,128)S(1)}) custom-call(f32[19,8,16,128]{3,2,1,0:T(8,128)S(1)} %copy-done, f32[3,8,16,128]{3,2,1,0:T(8,128)S(1)} %bitcast.5), custom_call_target="tpu_custom_call" | custom-call | tf_op jit(solution)/shard_map/fluid/pallas_call | solution.py:228
  38.2 14.7 %homeward.1 = f32[3,5136]{1,0:T(4,128)S(1)} custom-call(f32[8,33,128]{2,1,0:T(8,128)S(1)} %get-tuple-element.9.refs_0_, f32[384,128]{1,0:T(8,128)S(1)} %bitcast.4, s32[4,41,128]{2,1,0:T(8,128)S(1)} %get-tuple-element.11.refs_2_), custom_call_target="tpu_custom_call" | custom-call | tf_op jit(solution)/shard_map/homeward/pallas_call | solution.py:611
  53.0 1.0 %copy.10 = f32[19,8,16,128]{3,2,1,0:T(8,128)} copy(f32[19,8,16,128]{3,2,1,0:T(8,128)S(1)} %get-tuple-element.16) | data formatting | bytes 2490368
  54.0 0.6 %copy.11 = f32[3,5136]{1,0:T(4,128)} copy(f32[3,5136]{1,0:T(4,128)S(1)} %homeward.1) | data formatting | bytes 123264
  (3 shorter events, 0.1 us)
Async XLA Ops:
  0.6 3.3 %copy-start.1 = (s32[5136,1]{0,1:T(1,128)S(1)}, s32[5136,1]{0,1:T(1,128)}, u32[]{:S(2)}) copy-start(s32[5136,1]{0,1:T(1,128)} %param.11) | copy-start | bytes 61636
  0.6 28.0 %copy-start = (f32[19,8,16,128]{3,2,1,0:T(8,128)S(1)}, f32[19,8,16,128]{3,2,1,0:T(8,128)}, u32[]{:S(2)}) copy-start(f32[19,8,16,128]{3,2,1,0:T(8,128)} %populations_ref.1) | copy-start | bytes 3735556
